TPU v7x, 512 devices: a whole 4x4x16 slice. The times are simulated.
512 devices in a mesh: row: 32 (over z_lo, y, core), col: 16 (over z_hi, x).
Axes of the slice: x: 4, y: 4, z: 16 (z_hi: 4, z_lo: 4; z = z_hi * 4 + z_lo), core: 2. Of those that a mesh axis runs over, the one named last changes fastest.
Arguments:
- pair: bfloat16 [384, 384, 128], P('row', 'col'), may hold values from -6 to 6
- d_out: bfloat16 [384, 384, 128], P('row', 'col'), may hold values from -6 to 6
- w_proj: bfloat16 [128, 256], replicated, may hold values from -0.5 to 0.5
- w_gate: bfloat16 [128, 128], replicated, may hold values from -0.5 to 0.5
- output_weight: bfloat16 [64, 128], replicated, may hold values from -0.75 to 0.75
Outputs:
- d_pair: float32 [384, 384, 128], P('row', 'col')
All inputs are finite; a program needn't handle non-finite values.
Results may differ from a plain program's by a relative error of at most 0.0069.
Values may be sent and summed in bfloat16 or wider, within the bound.
A program may use at most 64 MiB of HBM per device.

v0:
```python
import jax
import jax.numpy as jnp
from jax import lax
from jax.sharding import PartitionSpec as P

EPS = 1e-05


def apply_layer_norm(values, reduce_dim):
    centre = values - jnp.mean(values, axis=reduce_dim, keepdims=True)
    inv_std = lax.rsqrt(jnp.mean(centre * centre, axis=reduce_dim, keepdims=True) + EPS)
    return (centre * inv_std, inv_std)


def layer_norm_backward(upstream, normed, inv_std, reduce_dim):
    grad_mean = jnp.mean(upstream, axis=reduce_dim, keepdims=True)
    cross_mean = jnp.mean(upstream * normed, axis=reduce_dim, keepdims=True)
    return (upstream - grad_mean - normed * cross_mean) * inv_std


def per_device(pair, d_out, w_proj, w_gate, output_weight):
    tile_rows, tile_cols, pair_width = pair.shape
    hidden_channels = output_weight.shape[0]
    pair_cell_count = tile_rows * tile_cols
    zhat, inv_std = apply_layer_norm(
        pair.astype(jnp.float32).reshape(pair_cell_count, pair_width), 1
    )
    normed = zhat.astype(jnp.bfloat16)
    projected = jnp.dot(normed, w_proj, preferred_element_type=jnp.float32)
    a_gate = jax.nn.sigmoid(projected[:, :hidden_channels])
    a_value = projected[:, hidden_channels : 2 * hidden_channels]
    b_gate = jax.nn.sigmoid(projected[:, 2 * hidden_channels : 3 * hidden_channels])
    b_value = projected[:, 3 * hidden_channels :]
    left_cells = (a_gate * a_value).astype(jnp.bfloat16)
    right_cells = (b_gate * b_value).astype(jnp.bfloat16)
    left_tile = jnp.transpose(left_cells.reshape(tile_rows, tile_cols, hidden_channels), (2, 0, 1))
    right_tile = jnp.transpose(
        right_cells.reshape(tile_rows, tile_cols, hidden_channels), (2, 0, 1)
    )
    left_panel = lax.all_gather(left_tile, "col", axis=2, tiled=True)
    right_columns = lax.all_gather(right_tile, "row", axis=1, tiled=True)
    right_panel = lax.all_to_all(right_columns, "col", split_axis=1, concat_axis=2, tiled=True)
    input_tile = jnp.einsum(
        "hik,hjk->hij", left_panel, right_panel, preferred_element_type=jnp.float32
    )
    standardized_tile, tile_inverse_std = apply_layer_norm(input_tile, 0)
    standardized_input = jnp.transpose(standardized_tile, (1, 2, 0)).reshape(
        pair_cell_count, hidden_channels
    )
    input_inverse_std = jnp.transpose(tile_inverse_std, (1, 2, 0)).reshape(pair_cell_count, 1)
    mixed_product = jnp.dot(
        standardized_input.astype(jnp.bfloat16), output_weight, preferred_element_type=jnp.float32
    )
    gate = jax.nn.sigmoid(jnp.dot(normed, w_gate, preferred_element_type=jnp.float32))
    upstream_out = d_out.reshape(pair_cell_count, pair_width).astype(jnp.float32)
    d_gate = (upstream_out * mixed_product * gate * (1.0 - gate)).astype(jnp.bfloat16)
    mixed_gradient = (upstream_out * gate).astype(jnp.bfloat16)
    standardized_gradient = jnp.dot(
        mixed_gradient, output_weight.T, preferred_element_type=jnp.float32
    )
    input_gradient = layer_norm_backward(
        standardized_gradient, standardized_input, input_inverse_std, 1
    ).astype(jnp.bfloat16)
    dx_tile = jnp.transpose(
        input_gradient.reshape(tile_rows, tile_cols, hidden_channels), (2, 0, 1)
    )
    left_terms = jnp.einsum(
        "hij,hjk->hik", dx_tile, right_panel, preferred_element_type=jnp.float32
    )
    d_left_tile = lax.psum_scatter(left_terms, "col", scatter_dimension=2, tiled=True)
    right_terms = jnp.einsum(
        "hij,hik->hjk", dx_tile, left_panel, preferred_element_type=jnp.float32
    )
    returned = lax.all_to_all(right_terms, "col", split_axis=2, concat_axis=1, tiled=True)
    d_right_tile = lax.psum_scatter(returned, "row", scatter_dimension=1, tiled=True)
    d_left = jnp.transpose(d_left_tile, (1, 2, 0)).reshape(pair_cell_count, hidden_channels)
    d_right = jnp.transpose(d_right_tile, (1, 2, 0)).reshape(pair_cell_count, hidden_channels)
    d_projected = jnp.concatenate(
        [
            d_left * a_value * a_gate * (1.0 - a_gate),
            d_left * a_gate,
            d_right * b_value * b_gate * (1.0 - b_gate),
            d_right * b_gate,
        ],
        axis=1,
    ).astype(jnp.bfloat16)
    d_normed = jnp.dot(d_projected, w_proj.T, preferred_element_type=jnp.float32) + jnp.dot(
        d_gate, w_gate.T, preferred_element_type=jnp.float32
    )
    d_pair = layer_norm_backward(d_normed, zhat, inv_std, 1)
    return d_pair.reshape(tile_rows, tile_cols, pair_width)


def solution(mesh):
    in_specs = (P("row", "col", None), P("row", "col", None), P(), P(), P())
    out_specs = P("row", "col", None)
    return jax.shard_map(
        per_device, mesh=mesh, in_specs=in_specs, out_specs=out_specs, check_vma=False
    )
```

profile of v0, /device:TPU:1, one launch (start us, length us, event | category | flops | bytes accessed | tf_op | source)
XLA Modules:
  0.0 634.2 jit_solution(11852023509415791841)
XLA Ops:
  6.5 0.0 copy-start
  6.5 0.0 all-gather.2.cloned.1.call-start
  6.5 1.0 convert_reduce_fusion
  7.6 0.1 div.36
  7.7 0.0 copy-start.11
  7.7 1.1 multiply_reduce_fusion.2
  8.8 0.1 rsqrt.27
  8.9 0.0 copy-start.13
  8.9 1.0 fusion.30
  9.9 0.0 copy-done
  9.9 0.0 copy-start.1
  9.9 0.2 fusion.37
  10.1 0.8 multiply_convert_fusion
  10.9 0.0 all-gather.2.cloned.1.call-update
  10.9 71.7 %all-gather.2.cloned.1.call-done = bf16[64,384,24]{0,2,1:T(8,128)(2,1)} async-done(((bf16[64,12,24]{0,2,1:T(8,128)(2,1)}), bf16[64,384,24]{0,2,1:T(8,128)(2,1)}) %all-gather.2.cloned.1.call-update) | async-done | bytes 1179664 | tf_op jit(solution)/shard_map/all_gather | solution.py:41
  82.6 4.9 reshape.108
  87.5 0.0 copy-done.11
  87.5 0.0 copy-done.13
  87.5 13.1 %all-to-all-start = ((bf16[16,2,18432]{2,1,0:T(2,128)(2,1)}), bf16[16,2,18432]{2,1,0:T(2,128)(2,1)}, u32[]{:S(2)}, u32[]{:S(2)}) async-start(bf16[16,2,18432]{2,1,0:T(2,128)(2,1)} %reshape.108), calls=%async_computation | async-start | bytes 2359296 | tf_op jit(solution)/shard_map/all_to_all | solution.py:42
  100.5 122.5 %all_gather.6 = bf16[64,12,384]{0,2,1:T(8,128)(2,1)S(1)} all-gather(bf16[64,12,24]{0,2,1:T(8,128)(2,1)S(1)} %bitcast.78), channel_id=1, replica_groups=mesh['row'=32,'col'=16] {'col'}, dimensions={2}, use_global_device_ids=true | all-gather | bytes 626688 | tf_op jit(solution)/shard_map/all_gather | solution.py:40
  223.0 1.0 copy.51
  224.1 0.8 fusion.2
  224.9 0.0 all-to-all-done
  224.9 4.0 reshape.109
  229.0 2.1 copy.50
  231.0 3.0 copy.52
  234.0 0.0 copy-start.7
  234.1 0.0 copy-start.9
  234.1 0.6 fusion.44
  234.6 0.1 multiply_reduce_fusion
  234.8 0.1 rsqrt.29
  234.9 0.2 copy.53
  235.1 0.1 copy.55
  235.2 1.1 fusion.43
  236.4 0.1 copy.56
  236.5 0.3 copy.57
  236.8 2.1 fusion.46
  238.9 5.0 copy.63
  243.8 5.9 reshape.110
  249.7 4.4 all-to-all-start.1
  254.2 0.0 reduce-scatter.3.cloned.1.call-start
  254.2 1.6 fusion.45
  255.8 3.3 copy.59
  259.1 0.0 reduce-scatter.3.cloned.1.call-update
  259.1 0.2 reduce-scatter.5.cloned.1.call-start
  259.4 110.8 %all-to-all-done.1 = f32[16,1,36864]{2,1,0:T(1,128)} async-done(((f32[16,1,36864]{2,1,0:T(1,128)}), f32[16,1,36864]{2,1,0:T(1,128)}, u32[]{:S(2)}, u32[]{:S(2)}) %all-to-all-start.1) | async-done | bytes 2359328 | tf_op jit(solution)/shard_map/all_to_all | solution.py:74
  370.2 0.6 broadcast.133
  370.8 8.1 %reduce.2 = f32[16,36864]{1,0:T(8,128)S(1)} reduce(f32[16,1,36864]{2,1,0:T(1,128)} %all-to-all-done.1, f32[]{:T(128)} %broadcast.133), dimensions={1}, to_apply=%all_to_all.30.reduce_sub_computation | reduce | bytes 4718596 | tf_op jit(solution)/shard_map/all_to_all | solution.py:74
  378.8 3.4 reshape.111
  382.2 5.3 copy.65
  387.5 0.0 reduce-scatter.5.cloned.1.call-update
  387.5 0.9 copy-done.4
  388.4 0.1 copy-done.6
  388.5 0.0 copy-done.8
  388.5 0.3 fusion.6
  388.8 85.5 %reduce-scatter.3.cloned.1.call-done = f32[64,12,24]{0,1,2:T(8,128)} async-done(((f32[64,12,384]{0,1,2:T(8,128)}), f32[64,12,24]{0,1,2:T(8,128)}) %reduce-scatter.3.cloned.1.call-update) | async-done | bytes 73744 | tf_op jit(solution)/shard_map/reduce_scatter | solution.py:70
  474.3 1.0 copy.60
  475.3 149.9 %reduce-scatter.5.cloned.1.call-done = f32[64,12,24]{0,2,1:T(8,128)} async-done(((f32[64,384,24]{0,2,1:T(8,128)}), f32[64,12,24]{0,2,1:T(8,128)}) %reduce-scatter.5.cloned.1.call-update) | async-done | bytes 73744 | tf_op jit(solution)/shard_map/reduce_scatter | solution.py:75
  625.2 1.1 fusion.28
  626.3 0.4 fusion.42
  626.7 0.0 copy-done.5
  626.7 0.0 copy-done.12
  626.7 0.0 copy-done.14
  626.7 0.9 subtract_multiply_fusion
  (24 shorter events, 0.1 us)
Async XLA Ops:
  6.5 3.4 copy-start
  6.5 76.0 %all-gather.2.cloned.1.call-start = ((), (), s32[]{:S(2)}) async-start(), calls=%async_computation.4 | async-start | bytes 2433024 | tf_op jit(solution)/shard_map/all_gather | solution.py:41
  7.7 79.8 %copy-start.11 = (f32[288]{0:T(512)}, f32[288]{0:T(512)S(1)}, u32[]{:S(2)}) copy-start(f32[288]{0:T(512)S(1)} %div.36) | copy-start | bytes 3460
  8.9 78.6 %copy-start.13 = (f32[288]{0:T(512)}, f32[288]{0:T(512)S(1)}, u32[]{:S(2)}) copy-start(f32[288]{0:T(512)S(1)} %rsqrt.27) | copy-start | bytes 3460
  9.9 214.2 %copy-start.1 = (f32[288,128]{1,0:T(8,128)}, f32[288,128]{1,0:T(8,128)S(1)}, u32[]{:S(2)}) copy-start(f32[288,128]{1,0:T(8,128)S(1)} %fusion.30) | copy-start | bytes 442372
  87.5 136.6 %copy-start.10 = (bf16[128,128]{1,0:T(8,128)(2,1)S(1)}, bf16[128,128]{1,0:T(8,128)(2,1)}, u32[]{:S(2)}) copy-start(bf16[128,128]{1,0:T(8,128)(2,1)} %param.8) | copy-start | bytes 98308
  87.5 137.5 %all-to-all-start = ((bf16[16,2,18432]{2,1,0:T(2,128)(2,1)}), bf16[16,2,18432]{2,1,0:T(2,128)(2,1)}, u32[]{:S(2)}, u32[]{:S(2)}) async-start(bf16[16,2,18432]{2,1,0:T(2,128)(2,1)} %reshape.108), calls=%async_computation | async-start | bytes 2359296 | tf_op jit(solution)/shard_map/all_to_all | solution.py:42
  234.0 1.2 copy-start.7
  234.1 1.2 copy-start.9
  235.1 1.4 copy-start.3
  249.7 120.4 %all-to-all-start.1 = ((f32[16,1,36864]{2,1,0:T(1,128)}), f32[16,1,36864]{2,1,0:T(1,128)}, u32[]{:S(2)}, u32[]{:S(2)}) async-start(f32[16,1,36864]{2,1,0:T(1,128)} %reshape.110), calls=%async_computation.2 | async-start | bytes 4718592 | tf_op jit(solution)/shard_map/all_to_all | solution.py:74
  254.2 220.1 %reduce-scatter.3.cloned.1.call-start = ((), (), s32[]{:S(2)}) async-start(), calls=%async_computation.5 | async-start | bytes 3342336 | tf_op jit(solution)/shard_map/reduce_scatter | solution.py:70
  259.1 366.1 %reduce-scatter.5.cloned.1.call-start = ((), (), s32[]{:S(2)}) async-start(), calls=%async_computation.6 | async-start | bytes 4866048 | tf_op jit(solution)/shard_map/reduce_scatter | solution.py:75
  387.5 0.9 copy-start.4
  387.5 1.0 copy-start.6
  387.5 1.0 copy-start.8
  387.5 238.8 %copy-start.2 = (f32[288,128]{1,0:T(8,128)S(1)}, f32[288,128]{1,0:T(8,128)}, u32[]{:S(2)}) copy-start(f32[288,128]{1,0:T(8,128)} %copy-done.1) | copy-start | bytes 442372
  388.5 238.2 %copy-start.5 = (bf16[12,24,128]{2,1,0:T(8,128)(2,1)S(1)}, bf16[12,24,128]{2,1,0:T(8,128)(2,1)}, u32[]{:S(2)}) copy-start(bf16[12,24,128]{2,1,0:T(8,128)(2,1)} %param.5) | copy-start | bytes 221188
  388.5 238.2 %copy-start.12 = (f32[288]{0:T(512)S(1)}, f32[288]{0:T(512)}, u32[]{:S(2)}) copy-start(f32[288]{0:T(512)} %copy-done.11) | copy-start | bytes 3460
  388.5 238.2 %copy-start.14 = (f32[288]{0:T(512)S(1)}, f32[288]{0:T(512)}, u32[]{:S(2)}) copy-start(f32[288]{0:T(512)} %copy-done.13) | copy-start | bytes 3460
Sparse Core Ops, SparseCore 0:
  11.0 71.5 all-gather.1
  259.3 215.0 reduce-scatter.2
  477.2 147.9 reduce-scatter.4
where the time goes:
time: 639 us; the launch traced here: 634 us
  waiting for transfers between devices  418 us (65%)
  blocking collectives  122 us (19%)
  local copies, waits for them, and re-layouts  41.4 us (6%)
  starting transfers between devices  17.8 us (3%)
  other arithmetic  14.1 us (2%)
  between operations  13.4 us (2%)
  matrix products  7.03 us (1%)
    reduce_scatter x1, waiting for transfers between devices, per_device(): lax.psum_scatter(returned, 'row', scatter_dimension=1, tiled=True)  150 us
    all_gather x1, blocking collectives, per_device(): left_panel = lax.all_gather(left_tile, 'col', axis=2, tiled=True)  122 us
    all_to_all x1, waiting for transfers between devices, per_device(): lax.all_to_all(right_terms, 'col', split_axis=2, concat_axis=1, tiled=True)  111 us
    reduce_scatter x1, waiting for transfers between devices, per_device(): lax.psum_scatter(left_terms, 'col', scatter_dimension=2, tiled=True)  85.5 us
    all_gather x1, waiting for transfers between devices, per_device(): right_columns = lax.all_gather(right_tile, 'row', axis=1, tiled=True)  71.7 us
    unnamed x34, local copies, waits for them, and re-layouts  19.2 us
    all_to_all x1, starting transfers between devices, per_device(): lax.all_to_all(right_columns, 'col', split_axis=1, concat_axis=2, tiled=T...  13.1 us
  transfers between devices with their start and end apart: 5, of which 4 were waited for; matrix products, arithmetic and copies ran while one was open for 4% of the time, Pallas kernels for 0%

commit v1 on v0

v1 whole, which is shorter than its diff:
```python
import functools

import jax
import jax.numpy as jnp
from jax import lax
from jax.experimental import pallas as pl
from jax.experimental.pallas import tpu as pltpu
from jax.sharding import PartitionSpec as P

EPS = 1e-05
MESH = pl.DeviceIdType.MESH
F32 = jnp.float32
BF16 = jnp.bfloat16

ROWS = 32
COLS = 16
OWNERS = 4
OWNER_STEP = 10
HALF = 12
TILE_I = 12
LANES = 128


def dot(a, b):
    return lax.dot_general(a, b, (((1,), (0,)), ((), ())), preferred_element_type=F32)


def dot_t(a, b):
    return lax.dot_general(a, b, (((1,), (1,)), ((), ())), preferred_element_type=F32)


def swap_blocks(parts):
    lane = lax.broadcasted_iota(jnp.int32, parts[0].shape, 1)
    low = lane < 64
    even = (lane // 32) % 2 == 0
    p0, p1, p2, p3 = parts
    t0 = jnp.where(low, p0, pltpu.roll(p2, 64, 1))
    t2 = jnp.where(low, pltpu.roll(p0, 64, 1), p2)
    t1 = jnp.where(low, p1, pltpu.roll(p3, 64, 1))
    t3 = jnp.where(low, pltpu.roll(p1, 64, 1), p3)
    u0 = jnp.where(even, t0, pltpu.roll(t1, 32, 1))
    u1 = jnp.where(even, pltpu.roll(t0, 96, 1), t1)
    u2 = jnp.where(even, t2, pltpu.roll(t3, 32, 1))
    u3 = jnp.where(even, pltpu.roll(t2, 96, 1), t3)
    return u0, u1, u2, u3


def body(
    pair_ref, d_out_ref, w_proj_ref, w_gate_ref, ow_ref, out_ref,
    pad_ref, rows8_ref, rows4_ref, xs_ref,
    send_a, recv_a, send_b, recv_b, send_c, recv_c, send_d, recv_d,
    send_e, recv_e, send_f, recv_f, send_g, recv_g, send_h, recv_h,
    send_sem, recv_sem, quad_sem,
):
    r = lax.axis_index("row")
    c = lax.axis_index("col")
    is_owner = r % OWNER_STEP == 0
    barrier = pltpu.get_barrier_semaphore()

    def greet_col(d, carry):
        pl.semaphore_signal(barrier, inc=1, device_id=(r, lax.rem(c + d, COLS)), device_id_type=MESH)
        return carry

    lax.fori_loop(1, COLS, greet_col, 0)

    @pl.when(is_owner)
    def _():
        def greet_row(d, carry):
            pl.semaphore_signal(barrier, inc=1, device_id=(lax.rem(r + d, ROWS), c), device_id_type=MESH)
            return carry

        lax.fori_loop(1, ROWS, greet_row, 0)

    @pl.when(jnp.logical_not(is_owner))
    def _():
        for q in range(OWNERS):
            pl.semaphore_signal(barrier, inc=1, device_id=(q * OWNER_STEP, c), device_id_type=MESH)

    def padded_transpose(ref):
        for i in range(TILE_I):
            cells = ref[i].astype(F32)
            pad_ref[32 * i : 32 * i + HALF, :] = cells[:HALF]
            pad_ref[32 * i + 16 : 32 * i + 16 + HALF, :] = cells[HALF:]
        return pad_ref[...].T

    def all_to_all(phase, send, recv):
        pltpu.make_async_copy(send.at[c], recv.at[c], recv_sem.at[phase]).start()

        def one(d, carry):
            to = lax.rem(c + d, COLS)
            pltpu.make_async_remote_copy(
                src_ref=send.at[to], dst_ref=recv.at[c],
                send_sem=send_sem.at[phase], recv_sem=recv_sem.at[phase],
                device_id=(r, to), device_id_type=MESH,
            ).start()
            return carry

        lax.fori_loop(1, COLS, one, 0)

    def to_owners(phase, send, recv):
        for q in range(OWNERS):
            @pl.when(r == q * OWNER_STEP)
            def _():
                pltpu.make_async_copy(send.at[q], recv.at[r], recv_sem.at[phase]).start()

            @pl.when(r != q * OWNER_STEP)
            def _():
                pltpu.make_async_remote_copy(
                    src_ref=send.at[q], dst_ref=recv.at[r],
                    send_sem=quad_sem.at[phase, q], recv_sem=recv_sem.at[phase],
                    device_id=(q * OWNER_STEP, c), device_id_type=MESH,
                ).start()

    def from_owner(phase, send, recv):
        q = r // OWNER_STEP
        pltpu.make_async_copy(send.at[r], recv.at[q], quad_sem.at[phase, q]).start()

        def one(d, carry):
            to = lax.rem(r + d, ROWS)
            pltpu.make_async_remote_copy(
                src_ref=send.at[to], dst_ref=recv.at[q],
                send_sem=send_sem.at[phase], recv_sem=quad_sem.at[phase, q],
                device_id=(to, c), device_id_type=MESH,
            ).start()
            return carry

        lax.fori_loop(1, ROWS, one, 0)

    def wait_all(ref, sem):
        pltpu.make_async_copy(ref, ref, sem).wait()

    def wait_quads(phase, recv):
        for q in range(OWNERS):
            wait_all(recv.at[q], quad_sem.at[phase, q])

    def spread(recv, stage, rows):
        for z in range(4):
            for a in range(3):
                parts = [recv[4 * z + x, :, LANES * a : LANES * (a + 1)].astype(F32) for x in range(4)]
                for b, part in enumerate(swap_blocks(parts)):
                    stage[z, pl.ds(4 * a + b, rows, stride=16), :] = part

    def collect(stage, send, rows):
        for z in range(4):
            for a in range(3):
                parts = [stage[z, pl.ds(4 * a + b, rows, stride=16), :] for b in range(4)]
                for x, part in enumerate(swap_blocks(parts)):
                    send[4 * z + x, :, LANES * a : LANES * (a + 1)] = part.astype(BF16)

    pad_ref[...] = jnp.zeros_like(pad_ref)
    rows8_ref[...] = jnp.zeros_like(rows8_ref)
    rows4_ref[...] = jnp.zeros_like(rows4_ref)
    new = lax.broadcasted_iota(jnp.int32, (256, 256), 0)
    old = lax.broadcasted_iota(jnp.int32, (256, 256), 1)
    left_right = new % 2
    q_of = (new // 2) % 4
    col_of = (new // 8) % 16
    value = new // 128
    order = (old == left_right * 128 + value * 64 + col_of * 4 + q_of).astype(F32).astype(BF16)
    w_rows = dot_t(order, w_proj_ref[...]).astype(BF16)
    w_cols = dot_t(w_proj_ref[...], order).astype(BF16)
    eye = (
        lax.broadcasted_iota(jnp.int32, (128, 128), 0) == lax.broadcasted_iota(jnp.int32, (128, 128), 1)
    ).astype(F32).astype(BF16)
    w_gate_t = dot_t(eye, w_gate_ref[...]).astype(BF16)
    ow_t = dot_t(eye, ow_ref[...]).astype(BF16)

    values = padded_transpose(pair_ref)
    centre = values - jnp.mean(values, axis=0, keepdims=True)
    inv_std = lax.rsqrt(jnp.mean(centre * centre, axis=0, keepdims=True) + EPS)
    zhat = centre * inv_std
    normed = zhat.astype(BF16)
    projected = dot(w_rows, normed)
    gates = jax.nn.sigmoid(projected[:128])
    vals = projected[128:]
    send_a[...] = (gates * vals).astype(BF16).reshape(COLS, 8, 384)

    pl.semaphore_wait(barrier, COLS - 1 + jnp.where(is_owner, ROWS - 1, OWNERS))
    all_to_all(0, send_a, recv_a)

    upstream = padded_transpose(d_out_ref)
    gate = jax.nn.sigmoid(dot(w_gate_t, normed))
    d_xhat = dot(ow_ref[...], (upstream * gate).astype(BF16))
    d_xhat_mean = jnp.mean(d_xhat, axis=0, keepdims=True)
    gate_slope = upstream * gate * (1.0 - gate)

    wait_all(recv_a, recv_sem.at[0])
    spread(recv_a, rows8_ref, 8)
    for q in range(OWNERS):
        send_b[q] = rows8_ref[:, 32 * q : 32 * q + 32, :].astype(BF16)
    to_owners(1, send_b, recv_b)

    def matrix(recv, lo):
        return jnp.concatenate(
            [recv[:, z, lo : lo + 16, :].reshape(ROWS * 16, LANES) for z in range(4)], axis=1
        )

    def put(send, lo, product):
        for z in range(4):
            send[:, z, lo : lo + 16, :] = (
                product[:, LANES * z : LANES * (z + 1)].astype(BF16).reshape(ROWS, 16, LANES)
            )

    @pl.when(is_owner)
    def _():
        wait_all(recv_b, recv_sem.at[1])
        put(send_c, 0, dot_t(matrix(recv_b, 0), matrix(recv_b, 16)))
        from_owner(2, send_c, recv_c)

    wait_quads(2, recv_c)
    for z in range(4):
        rows4_ref[z] = recv_c[:, z].reshape(OWNERS * 16, LANES).astype(F32)
    collect(rows4_ref, send_d, 4)
    all_to_all(3, send_d, recv_d)
    wait_all(recv_d, recv_sem.at[3])
    for s in range(COLS):
        xs_ref[4 * s : 4 * s + 4, :] = recv_d[s].astype(F32)

    x = xs_ref[...]
    x_centre = x - jnp.mean(x, axis=0, keepdims=True)
    x_inv = lax.rsqrt(jnp.mean(x_centre * x_centre, axis=0, keepdims=True) + EPS)
    xhat = x_centre * x_inv
    d_x = (d_xhat - d_xhat_mean - xhat * jnp.mean(d_xhat * xhat, axis=0, keepdims=True)) * x_inv
    xs_ref[...] = d_x
    for s in range(COLS):
        send_e[s] = xs_ref[4 * s : 4 * s + 4, :].astype(BF16)
    all_to_all(4, send_e, recv_e)

    mixed = dot(ow_t, xhat.astype(BF16))
    d_gate = (mixed * gate_slope).astype(BF16)
    d_normed_gate = dot(w_gate_ref[...], d_gate)

    wait_all(recv_e, recv_sem.at[4])
    rows4_ref[...] = jnp.zeros_like(rows4_ref)
    spread(recv_e, rows4_ref, 4)
    for q in range(OWNERS):
        send_f[q] = rows4_ref[:, 16 * q : 16 * q + 16, :].astype(BF16)
    to_owners(5, send_f, recv_f)

    @pl.when(is_owner)
    def _():
        wait_all(recv_f, recv_sem.at[5])
        d_x_all = matrix(recv_f, 0)
        put(send_g, 0, dot(d_x_all, matrix(recv_b, 16)))
        put(send_g, 16, dot(d_x_all.astype(F32).T.astype(BF16), matrix(recv_b, 0)))
        from_owner(6, send_g, recv_g)

    wait_quads(6, recv_g)
    for z in range(4):
        rows8_ref[z] = recv_g[:, z].reshape(OWNERS * 32, LANES).astype(F32)
    collect(rows8_ref, send_h, 8)
    all_to_all(7, send_h, recv_h)
    wait_all(recv_h, recv_sem.at[7])

    d_lr = recv_h[...].astype(F32).reshape(COLS * 8, 384)
    d_vals = d_lr * gates
    d_gates = d_vals * vals * (1.0 - gates)
    d_projected = jnp.concatenate([d_gates.astype(BF16), d_vals.astype(BF16)], axis=0)
    d_normed = dot(w_cols, d_projected) + d_normed_gate
    grad_mean = jnp.mean(d_normed, axis=0, keepdims=True)
    cross_mean = jnp.mean(d_normed * zhat, axis=0, keepdims=True)
    pad_ref[...] = ((d_normed - grad_mean - zhat * cross_mean) * inv_std).T
    for i in range(TILE_I):
        out_ref[i, :HALF, :] = pad_ref[32 * i : 32 * i + HALF, :]
        out_ref[i, HALF:, :] = pad_ref[32 * i + 16 : 32 * i + 16 + HALF, :]

    for phase, send in ((0, send_a), (3, send_d), (4, send_e), (7, send_h)):
        wait_all(send.at[pl.ds(0, COLS - 1)], send_sem.at[phase])
    for phase, send in ((1, send_b), (5, send_f)):
        for q in range(OWNERS):
            @pl.when(r != q * OWNER_STEP)
            def _():
                wait_all(send.at[q], quad_sem.at[phase, q])

    @pl.when(is_owner)
    def _():
        for phase, send in ((2, send_c), (6, send_g)):
            wait_all(send.at[pl.ds(0, ROWS - 1)], send_sem.at[phase])


def per_device(pair, d_out, w_proj, w_gate, output_weight):
    vmem = pl.BlockSpec(memory_space=pltpu.VMEM)
    return pl.pallas_call(
        body,
        out_shape=jax.ShapeDtypeStruct(pair.shape, F32),
        in_specs=[vmem] * 5,
        out_specs=vmem,
        scratch_shapes=[
            pltpu.VMEM((384, LANES), F32),
            pltpu.VMEM((4, 128, LANES), F32),
            pltpu.VMEM((4, 64, LANES), F32),
            pltpu.VMEM((64, 384), F32),
            pltpu.VMEM((COLS, 8, 384), BF16),
            pltpu.VMEM((COLS, 8, 384), BF16),
            pltpu.VMEM((OWNERS, 4, 32, LANES), BF16),
            pltpu.VMEM((ROWS, 4, 32, LANES), BF16),
            pltpu.VMEM((ROWS, 4, 16, LANES), BF16),
            pltpu.VMEM((OWNERS, 4, 16, LANES), BF16),
            pltpu.VMEM((COLS, 4, 384), BF16),
            pltpu.VMEM((COLS, 4, 384), BF16),
            pltpu.VMEM((COLS, 4, 384), BF16),
            pltpu.VMEM((COLS, 4, 384), BF16),
            pltpu.VMEM((OWNERS, 4, 16, LANES), BF16),
            pltpu.VMEM((ROWS, 4, 16, LANES), BF16),
            pltpu.VMEM((ROWS, 4, 32, LANES), BF16),
            pltpu.VMEM((OWNERS, 4, 32, LANES), BF16),
            pltpu.VMEM((COLS, 8, 384), BF16),
            pltpu.VMEM((COLS, 8, 384), BF16),
            pltpu.SemaphoreType.DMA((8,)),
            pltpu.SemaphoreType.DMA((8,)),
            pltpu.SemaphoreType.DMA((8, OWNERS)),
        ],
        compiler_params=pltpu.CompilerParams(
            collective_id=0, has_side_effects=True, vmem_limit_bytes=48 * 1024 * 1024
        ),
    )(pair, d_out, w_proj, w_gate, output_weight)


def solution(mesh):
    return jax.shard_map(
        per_device,
        mesh=mesh,
        in_specs=(P("row", "col", None), P("row", "col", None), P(), P(), P()),
        out_specs=P("row", "col", None),
        check_vma=False,
    )
```

time: 639 us -> 94.2 us (0.15)
  the two profiles are of different devices: /device:TPU:1 before, /device:TPU:120 now
where the time goes in v1:
time: 94.2 us; the launch traced here: 93.8 us
  Pallas kernels  89.1 us (95%)
  local copies, waits for them, and re-layouts  4.74 us (5%)
    pallas_call x1, Pallas kernels, per_device(): pl.pallas_call(body, out_shape=jax.ShapeDtypeStruct(pair.shape, F32), in_...  89.1 us
    unnamed x11, local copies, waits for them, and re-layouts  4.74 us

profile of v1, /device:TPU:120, one launch (start us, length us, event | category | flops | bytes accessed | tf_op | source)
XLA Modules:
  0.0 93.8 jit_solution(7168297825392694022)
XLA Ops:
  0.0 0.0 copy-start
  0.0 0.9 copy-done
  0.9 0.0 copy-start.1
  0.9 0.9 copy-done.1
  1.8 0.0 copy-start.2
  1.8 0.8 copy-done.2
  2.6 0.0 copy-start.3
  2.6 0.8 copy-done.3
  3.4 0.0 copy-start.4
  3.4 0.7 copy-done.4
  4.1 89.1 %shard_map.55 = f32[12,24,128]{2,1,0:T(8,128)S(1)} custom-call(bf16[12,24,128]{2,1,0:T(8,128)(2,1)S(1)} %copy-done, bf16[12,24,128]{2,1,0:T(8,128)(2,1)S(1)} %copy-done.1, bf16[128,256]{1,0:T(8,128)(2,1)S(1)} %copy-done.2, bf16[128,128]{1,0:T(8,128)(2,1)S(1)} %copy-done.3, bf16[64,128]{1,0:T(8,128)(2,1)S(1)} %copy-done.4), custom_call_target="tpu_custom_call" | custom-call | tf_op jit(solution)/shard_map/pallas_call | solution.py:283
  93.2 0.7 copy.7
Async XLA Ops:
  0.0 0.9 copy-start
  0.9 0.9 copy-start.1
  1.8 0.8 copy-start.2
  2.6 0.8 copy-start.3
  3.4 0.7 copy-start.4

commit v2 on v1

v2 whole, which is shorter than its diff:
```python
import functools

import jax
import jax.numpy as jnp
from jax import lax
from jax.experimental import pallas as pl
from jax.experimental.pallas import tpu as pltpu
from jax.sharding import PartitionSpec as P

EPS = 1e-05
MESH = pl.DeviceIdType.MESH
F32 = jnp.float32
BF16 = jnp.bfloat16

ROWS = 32
COLS = 16
OWNERS = 4
BLOCK = 8
HALF = 12
TILE_I = 12
LANES = 128


def dot(a, b):
    return lax.dot_general(a, b, (((1,), (0,)), ((), ())), preferred_element_type=F32)


def dot_t(a, b):
    return lax.dot_general(a, b, (((1,), (1,)), ((), ())), preferred_element_type=F32)


def swap_blocks(parts):
    lane = lax.broadcasted_iota(jnp.int32, parts[0].shape, 1)
    low = lane < 64
    even = (lane // 32) % 2 == 0
    p0, p1, p2, p3 = parts
    t0 = jnp.where(low, p0, pltpu.roll(p2, 64, 1))
    t2 = jnp.where(low, pltpu.roll(p0, 64, 1), p2)
    t1 = jnp.where(low, p1, pltpu.roll(p3, 64, 1))
    t3 = jnp.where(low, pltpu.roll(p1, 64, 1), p3)
    u0 = jnp.where(even, t0, pltpu.roll(t1, 32, 1))
    u1 = jnp.where(even, pltpu.roll(t0, 96, 1), t1)
    u2 = jnp.where(even, t2, pltpu.roll(t3, 32, 1))
    u3 = jnp.where(even, pltpu.roll(t2, 96, 1), t3)
    return u0, u1, u2, u3


def close_gaps(tiles):
    place = lax.broadcasted_iota(jnp.int32, tiles[0].shape, 1) % 16
    return [
        jnp.where(place < HALF, tiles[t], pltpu.roll(tiles[3], HALF - 4 * t, 1)) for t in range(3)
    ]


def open_gaps(tiles):
    place = lax.broadcasted_iota(jnp.int32, tiles[0].shape, 1) % 16
    back = [pltpu.roll(tiles[t], LANES - HALF + 4 * t, 1) for t in range(3)]
    return list(tiles) + [jnp.where(place < 4, back[0], jnp.where(place < 8, back[1], back[2]))]


def body(
    pair_hbm, d_out_hbm, w_proj_hbm, w_gate_hbm, ow_hbm, out_ref,
    pair_ref, d_out_ref, w_proj_ref, w_gate_ref, ow_ref,
    pad_ref, rows8_ref, rows4_ref, xs_ref, tiles_ref,
    send_a, recv_a, send_b, recv_l, recv_r, send_c, recv_c, send_d, recv_d,
    send_e, recv_e, send_f, send_fz, recv_f, recv_fz, send_g, recv_g, send_h, recv_h,
    in_sem, send_sem, recv_sem, near_sem, far_sem, near_recv, far_recv,
):
    r = lax.axis_index("row")
    c = lax.axis_index("col")
    z_me = r // BLOCK
    q_me = (r // 2) % OWNERS
    is_owner = r % 2 == 0
    not_owner = jnp.logical_not(is_owner)
    barrier = pltpu.get_barrier_semaphore()

    loads = [
        pltpu.make_async_copy(src, dst, in_sem.at[n])
        for n, (src, dst) in enumerate((
            (pair_hbm, pair_ref), (w_proj_hbm, w_proj_ref), (d_out_hbm, d_out_ref),
            (w_gate_hbm, w_gate_ref), (ow_hbm, ow_ref),
        ))
    ]
    for load in loads:
        load.start()

    def greet_col(d, carry):
        pl.semaphore_signal(barrier, inc=1, device_id=(r, lax.rem(c + d, COLS)), device_id_type=MESH)
        return carry

    lax.fori_loop(1, COLS, greet_col, 0)

    @pl.when(is_owner)
    def _():
        def greet_row(d, carry):
            pl.semaphore_signal(barrier, inc=1, device_id=(lax.rem(r + d, ROWS), c), device_id_type=MESH)
            return carry

        lax.fori_loop(1, ROWS, greet_row, 0)

    @pl.when(not_owner)
    def _():
        def greet_owner(n, carry):
            pl.semaphore_signal(barrier, inc=1, device_id=(2 * n, c), device_id_type=MESH)
            return carry

        lax.fori_loop(0, ROWS // 2, greet_owner, 0)

    def padded_transpose(ref):
        for i in range(TILE_I):
            cells = ref[i].astype(F32)
            pad_ref[32 * i : 32 * i + HALF, :] = cells[:HALF]
            pad_ref[32 * i + 16 : 32 * i + 16 + HALF, :] = cells[HALF:]
        return pad_ref[...].T

    def all_to_all(phase, send, recv):
        def one(dz, dx):
            to = lax.rem(c // 4 + dz, 4) * 4 + lax.rem(c + dx, 4)
            pltpu.make_async_remote_copy(
                src_ref=send.at[to], dst_ref=recv.at[c],
                send_sem=send_sem.at[phase], recv_sem=recv_sem.at[phase],
                device_id=(r, to), device_id_type=MESH,
            ).start()

        def opposite(n, carry):
            one(2, n)
            return carry

        def beside(n, carry):
            one(1 + 2 * (n % 2), n // 2)
            return carry

        def same(n, carry):
            one(0, n)
            return carry

        lax.fori_loop(0, 4, opposite, 0)
        lax.fori_loop(0, 8, beside, 0)
        lax.fori_loop(1, 4, same, 0)
        pltpu.make_async_copy(send.at[c], recv.at[c], recv_sem.at[phase]).start()

    def to_near_owners(phase, src_of, dst):
        for q in range(OWNERS):
            owner = z_me * BLOCK + 2 * q

            @pl.when(r == owner)
            def _():
                pltpu.make_async_copy(src_of(q), dst, near_recv.at[phase]).start()

            @pl.when(r != owner)
            def _():
                pltpu.make_async_remote_copy(
                    src_ref=src_of(q), dst_ref=dst,
                    send_sem=near_sem.at[phase, q], recv_sem=near_recv.at[phase],
                    device_id=(owner, c), device_id_type=MESH,
                ).start()

    def to_far_owners(phase, src_of, dst):
        for dz in (3, 1, 2):
            z = lax.rem(z_me + dz, 4)
            for q in range(OWNERS):
                pltpu.make_async_remote_copy(
                    src_ref=src_of(q, z), dst_ref=dst,
                    send_sem=far_sem.at[phase], recv_sem=far_recv.at[phase],
                    device_id=(z * BLOCK + 2 * q, c), device_id_type=MESH,
                ).start()

    def from_owner(phase, send, recv):
        me = r % BLOCK
        pltpu.make_async_copy(send.at[me], recv.at[q_me], near_sem.at[phase, q_me]).start()

        def one(d, carry):
            to = lax.rem(me + d, BLOCK)
            pltpu.make_async_remote_copy(
                src_ref=send.at[to], dst_ref=recv.at[q_me],
                send_sem=send_sem.at[phase], recv_sem=near_sem.at[phase, q_me],
                device_id=(z_me * BLOCK + to, c), device_id_type=MESH,
            ).start()
            return carry

        lax.fori_loop(1, BLOCK, one, 0)

    def wait_all(ref, sem):
        pltpu.make_async_copy(ref, ref, sem).wait()

    def wait_quads(phase, recv):
        for q in range(OWNERS):
            wait_all(recv.at[q], near_sem.at[phase, q])

    def wait_near_sends(phase, src_of):
        for q in range(OWNERS):
            @pl.when(r != z_me * BLOCK + 2 * q)
            def _():
                wait_all(src_of(q), near_sem.at[phase, q])

    def spread(recv, stage, rows):
        for z in range(4):
            for a in range(3):
                parts = [recv[4 * z + x, :, LANES * a : LANES * (a + 1)].astype(F32) for x in range(4)]
                for b, part in enumerate(swap_blocks(parts)):
                    stage[z, pl.ds(4 * a + b, rows, stride=16), :] = part

    def collect(stage, send, rows):
        for z in range(4):
            for a in range(3):
                parts = [stage[z, pl.ds(4 * a + b, rows, stride=16), :] for b in range(4)]
                for x, part in enumerate(swap_blocks(parts)):
                    send[4 * z + x, :, LANES * a : LANES * (a + 1)] = part.astype(BF16)

    pad_ref[...] = jnp.zeros_like(pad_ref)
    rows8_ref[...] = jnp.zeros_like(rows8_ref)
    rows4_ref[...] = jnp.zeros_like(rows4_ref)
    new = lax.broadcasted_iota(jnp.int32, (256, 256), 0)
    old = lax.broadcasted_iota(jnp.int32, (256, 256), 1)
    left_right = new % 2
    q_of = (new // 2) % 4
    col_of = (new // 8) % 16
    value = new // 128
    order = (old == left_right * 128 + value * 64 + col_of * 4 + q_of).astype(F32).astype(BF16)
    eye = (
        lax.broadcasted_iota(jnp.int32, (128, 128), 0) == lax.broadcasted_iota(jnp.int32, (128, 128), 1)
    ).astype(F32).astype(BF16)

    loads[0].wait()
    values = padded_transpose(pair_ref)
    centre = values - jnp.mean(values, axis=0, keepdims=True)
    inv_std = lax.rsqrt(jnp.mean(centre * centre, axis=0, keepdims=True) + EPS)
    zhat = centre * inv_std
    normed = zhat.astype(BF16)
    loads[1].wait()
    w_rows = dot_t(order, w_proj_ref[...]).astype(BF16)
    projected = dot(w_rows, normed)
    gates = jax.nn.sigmoid(projected[:128])
    vals = projected[128:]
    send_a[...] = (gates * vals).astype(BF16).reshape(COLS, 8, 384)

    pl.semaphore_wait(barrier, COLS - 1 + jnp.where(is_owner, ROWS - 1, ROWS // 2))
    all_to_all(0, send_a, recv_a)

    for load in loads[2:]:
        load.wait()
    w_cols = dot_t(w_proj_ref[...], order).astype(BF16)
    w_gate_t = dot_t(eye, w_gate_ref[...]).astype(BF16)
    ow_t = dot_t(eye, ow_ref[...]).astype(BF16)
    upstream = padded_transpose(d_out_ref)
    gate = jax.nn.sigmoid(dot(w_gate_t, normed))
    d_xhat = dot(ow_ref[...], (upstream * gate).astype(BF16))
    d_xhat_mean = jnp.mean(d_xhat, axis=0, keepdims=True)
    gate_slope = upstream * gate * (1.0 - gate)

    wait_all(recv_a, recv_sem.at[0])
    spread(recv_a, rows8_ref, 8)
    for t, tile in enumerate(close_gaps([rows8_ref[z] for z in range(4)])):
        send_b[:, :, t] = tile.astype(BF16).reshape(OWNERS, 2, 16, LANES)
    to_far_owners(0, lambda q, z: send_b.at[q, 1], recv_r.at[r])
    to_near_owners(0, lambda q: send_b.at[q, 1], recv_r.at[r])
    to_near_owners(1, lambda q: send_b.at[q, 0], recv_l.at[r])
    to_far_owners(1, lambda q, z: send_b.at[q, 0], recv_l.at[r])

    def matrix(ref):
        count = ref.shape[0]
        return jnp.concatenate([ref[:, t].reshape(count * 16, LANES) for t in range(3)], axis=1)

    near = pl.ds(pl.multiple_of(z_me * BLOCK, BLOCK), BLOCK)
    others = pl.ds(0, ROWS - BLOCK)

    @pl.when(is_owner)
    def _():
        wait_all(recv_l.at[near], near_recv.at[1])
        wait_all(recv_r.at[near], near_recv.at[0])
        wait_all(recv_r.at[others], far_recv.at[0])
        x_rows = dot_t(matrix(recv_l.at[near]), matrix(recv_r))
        for t, tile in enumerate(close_gaps([x_rows[:, LANES * z : LANES * (z + 1)] for z in range(4)])):
            send_c[:, t] = tile.astype(BF16).reshape(BLOCK, 16, LANES)
        from_owner(2, send_c, recv_c)

    wait_all(send_a.at[pl.ds(0, COLS - 1)], send_sem.at[0])
    wait_quads(2, recv_c)
    tiles = [recv_c[:, t].reshape(OWNERS * 16, LANES).astype(F32) for t in range(3)]
    for z, tile in enumerate(open_gaps(tiles)):
        rows4_ref[z] = tile
    collect(rows4_ref, send_d, 4)
    all_to_all(3, send_d, recv_d)
    wait_near_sends(0, lambda q: send_b.at[q, 1])
    wait_near_sends(1, lambda q: send_b.at[q, 0])
    wait_all(recv_d, recv_sem.at[3])
    for s in range(COLS):
        xs_ref[4 * s : 4 * s + 4, :] = recv_d[s].astype(F32)

    x = xs_ref[...]
    x_centre = x - jnp.mean(x, axis=0, keepdims=True)
    x_inv = lax.rsqrt(jnp.mean(x_centre * x_centre, axis=0, keepdims=True) + EPS)
    xhat = x_centre * x_inv
    d_x = (d_xhat - d_xhat_mean - xhat * jnp.mean(d_xhat * xhat, axis=0, keepdims=True)) * x_inv
    xs_ref[...] = d_x
    for s in range(COLS):
        send_e[s] = xs_ref[4 * s : 4 * s + 4, :].astype(BF16)
    all_to_all(4, send_e, recv_e)

    mixed = dot(ow_t, xhat.astype(BF16))
    d_gate = (mixed * gate_slope).astype(BF16)
    d_normed_gate = dot(w_gate_ref[...], d_gate)
    rows4_ref[...] = jnp.zeros_like(rows4_ref)
    wait_all(send_d.at[pl.ds(0, COLS - 1)], send_sem.at[3])

    wait_all(recv_e, recv_sem.at[4])
    spread(recv_e, rows4_ref, 4)
    for z in range(4):
        send_fz[:, z] = rows4_ref[z].astype(BF16).reshape(OWNERS, 16, LANES)
    for t, tile in enumerate(close_gaps([rows4_ref[z] for z in range(4)])):
        send_f[:, t] = tile.astype(BF16).reshape(OWNERS, 16, LANES)
    to_far_owners(5, lambda q, z: send_fz.at[q, z], recv_fz.at[r])
    to_near_owners(5, lambda q: send_f.at[q], recv_f.at[r % BLOCK])

    @pl.when(is_owner)
    def _():
        wait_all(recv_f, near_recv.at[5])
        tiles = [recv_f[:, t].reshape(BLOCK * 16, LANES).astype(F32) for t in range(3)]
        wide = open_gaps(tiles)
        for z, tile in enumerate(wide):
            tiles_ref[z] = tile
        d_left = dot(jnp.concatenate(wide, axis=1).astype(BF16), matrix(recv_r))
        recv_fz[near] = tiles_ref[z_me].astype(BF16).reshape(BLOCK, 16, LANES)
        for t in range(3):
            send_g[:, 0, t] = d_left[:, LANES * t : LANES * (t + 1)].astype(BF16).reshape(BLOCK, 16, LANES)
        wait_all(recv_l.at[others], far_recv.at[1])
        wait_all(recv_fz.at[others], far_recv.at[5])
        d_x_t = recv_fz[...].reshape(ROWS * 16, LANES).astype(F32).T.astype(BF16)
        d_right = dot(d_x_t, matrix(recv_l))
        for t in range(3):
            send_g[:, 1, t] = d_right[:, LANES * t : LANES * (t + 1)].astype(BF16).reshape(BLOCK, 16, LANES)
        from_owner(6, send_g, recv_g)

    wait_all(send_e.at[pl.ds(0, COLS - 1)], send_sem.at[4])
    wait_all(recv_r.at[pl.ds(0, 12)], far_sem.at[0])
    wait_all(recv_l.at[pl.ds(0, 12)], far_sem.at[1])
    wait_quads(6, recv_g)
    tiles = [recv_g[:, :, t].reshape(OWNERS * 32, LANES).astype(F32) for t in range(3)]
    for z, tile in enumerate(open_gaps(tiles)):
        rows8_ref[z] = tile
    collect(rows8_ref, send_h, 8)
    all_to_all(7, send_h, recv_h)

    wait_near_sends(5, lambda q: send_f.at[q])
    wait_all(recv_fz.at[pl.ds(0, 12)], far_sem.at[5])

    @pl.when(is_owner)
    def _():
        for phase, send in ((2, send_c), (6, send_g)):
            wait_all(send.at[pl.ds(0, BLOCK - 1)], send_sem.at[phase])

    wait_all(recv_h, recv_sem.at[7])

    d_lr = recv_h[...].astype(F32).reshape(COLS * 8, 384)
    d_vals = d_lr * gates
    d_gates = d_vals * vals * (1.0 - gates)
    d_projected = jnp.concatenate([d_gates.astype(BF16), d_vals.astype(BF16)], axis=0)
    d_normed = dot(w_cols, d_projected) + d_normed_gate
    grad_mean = jnp.mean(d_normed, axis=0, keepdims=True)
    cross_mean = jnp.mean(d_normed * zhat, axis=0, keepdims=True)
    pad_ref[...] = ((d_normed - grad_mean - zhat * cross_mean) * inv_std).T
    for i in range(TILE_I):
        out_ref[i, :HALF, :] = pad_ref[32 * i : 32 * i + HALF, :]
        out_ref[i, HALF:, :] = pad_ref[32 * i + 16 : 32 * i + 16 + HALF, :]
    wait_all(send_h.at[pl.ds(0, COLS - 1)], send_sem.at[7])


def per_device(pair, d_out, w_proj, w_gate, output_weight):
    stage1_wide = pltpu.VMEM((COLS, 8, 384), BF16)
    stage1_slim = pltpu.VMEM((COLS, 4, 384), BF16)
    args = (pair, d_out, w_proj, w_gate, output_weight)
    return pl.pallas_call(
        body,
        out_shape=jax.ShapeDtypeStruct(pair.shape, F32),
        in_specs=[pl.BlockSpec(memory_space=pl.ANY)] * 5,
        out_specs=pl.BlockSpec(memory_space=pltpu.VMEM),
        scratch_shapes=[
            *(pltpu.VMEM(a.shape, a.dtype) for a in args),
            pltpu.VMEM((384, LANES), F32),
            pltpu.VMEM((4, 128, LANES), F32),
            pltpu.VMEM((4, 64, LANES), F32),
            pltpu.VMEM((64, 384), F32),
            pltpu.VMEM((4, 128, LANES), F32),
            stage1_wide,
            stage1_wide,
            pltpu.VMEM((OWNERS, 2, 3, 16, LANES), BF16),
            pltpu.VMEM((ROWS, 3, 16, LANES), BF16),
            pltpu.VMEM((ROWS, 3, 16, LANES), BF16),
            pltpu.VMEM((BLOCK, 3, 16, LANES), BF16),
            pltpu.VMEM((OWNERS, 3, 16, LANES), BF16),
            stage1_slim,
            stage1_slim,
            stage1_slim,
            stage1_slim,
            pltpu.VMEM((OWNERS, 3, 16, LANES), BF16),
            pltpu.VMEM((OWNERS, 4, 16, LANES), BF16),
            pltpu.VMEM((BLOCK, 3, 16, LANES), BF16),
            pltpu.VMEM((ROWS, 16, LANES), BF16),
            pltpu.VMEM((BLOCK, 2, 3, 16, LANES), BF16),
            pltpu.VMEM((OWNERS, 2, 3, 16, LANES), BF16),
            stage1_wide,
            stage1_wide,
            pltpu.SemaphoreType.DMA((5,)),
            pltpu.SemaphoreType.DMA((8,)),
            pltpu.SemaphoreType.DMA((8,)),
            pltpu.SemaphoreType.DMA((8, OWNERS)),
            pltpu.SemaphoreType.DMA((8,)),
            pltpu.SemaphoreType.DMA((8,)),
            pltpu.SemaphoreType.DMA((8,)),
        ],
        compiler_params=pltpu.CompilerParams(
            collective_id=0, has_side_effects=True, vmem_limit_bytes=48 * 1024 * 1024
        ),
    )(*args)


def solution(mesh):
    return jax.shard_map(
        per_device,
        mesh=mesh,
        in_specs=(P("row", "col", None), P("row", "col", None), P(), P(), P()),
        out_specs=P("row", "col", None),
        check_vma=False,
    )
```

time: 94.2 us -> 83.5 us (0.89)
  the two profiles are of different devices: /device:TPU:120 before, /device:TPU:1 now
where the time goes in v2:
time: 83.5 us; the launch traced here: 83.1 us
  Pallas kernels  78.3 us (94%)
  local copies, waits for them, and re-layouts  4.74 us (6%)
    pallas_call x1, Pallas kernels, per_device(): pl.pallas_call(body, out_shape=jax.ShapeDtypeStruct(pair.shape, F32), in_...  78.3 us
    unnamed x11, local copies, waits for them, and re-layouts  4.74 us

profile of v2, /device:TPU:1, one launch (start us, length us, event | category | flops | bytes accessed | tf_op | source)
XLA Modules:
  0.0 83.1 jit_solution(3245051834767291935)
XLA Ops:
  0.0 0.0 copy-start
  0.0 0.9 %copy-done = bf16[12,24,128]{2,1,0:T(8,128)(2,1)S(1)} copy-done((bf16[12,24,128]{2,1,0:T(8,128)(2,1)S(1)}, bf16[12,24,128]{2,1,0:T(8,128)(2,1)}, u32[]{:S(2)}) %copy-start) | copy-done | bytes 73752
  0.9 0.0 copy-start.1
  0.9 0.9 %copy-done.1 = bf16[12,24,128]{2,1,0:T(8,128)(2,1)S(1)} copy-done((bf16[12,24,128]{2,1,0:T(8,128)(2,1)S(1)}, bf16[12,24,128]{2,1,0:T(8,128)(2,1)}, u32[]{:S(2)}) %copy-start.1) | copy-done | bytes 73752
  1.8 0.0 copy-start.2
  1.8 0.8 %copy-done.2 = bf16[128,256]{1,0:T(8,128)(2,1)S(1)} copy-done((bf16[128,256]{1,0:T(8,128)(2,1)S(1)}, bf16[128,256]{1,0:T(8,128)(2,1)}, u32[]{:S(2)}) %copy-start.2) | copy-done | bytes 65560
  2.6 0.0 copy-start.3
  2.6 0.8 copy-done.3
  3.4 0.0 copy-start.4
  3.4 0.7 copy-done.4
  4.1 78.3 %shard_map.55 = f32[12,24,128]{2,1,0:T(8,128)S(1)} custom-call(bf16[12,24,128]{2,1,0:T(8,128)(2,1)S(1)} %copy-done, bf16[12,24,128]{2,1,0:T(8,128)(2,1)S(1)} %copy-done.1, bf16[128,256]{1,0:T(8,128)(2,1)S(1)} %copy-done.2, bf16[128,128]{1,0:T(8,128)(2,1)S(1)} %copy-done.3, bf16[64,128]{1,0:T(8,128)(2,1)S(1)} %copy-done.4), custom_call_target="tpu_custom_call" | custom-call | tf_op jit(solution)/shard_map/pallas_call | solution.py:372
  82.4 0.7 copy.7
Async XLA Ops:
  0.0 0.9 %copy-start = (bf16[12,24,128]{2,1,0:T(8,128)(2,1)S(1)}, bf16[12,24,128]{2,1,0:T(8,128)(2,1)}, u32[]{:S(2)}) copy-start(bf16[12,24,128]{2,1,0:T(8,128)(2,1)} %pair_hbm.1) | copy-start | bytes 221188
  0.9 0.9 %copy-start.1 = (bf16[12,24,128]{2,1,0:T(8,128)(2,1)S(1)}, bf16[12,24,128]{2,1,0:T(8,128)(2,1)}, u32[]{:S(2)}) copy-start(bf16[12,24,128]{2,1,0:T(8,128)(2,1)} %d_out_hbm.1) | copy-start | bytes 221188
  1.8 0.8 %copy-start.2 = (bf16[128,256]{1,0:T(8,128)(2,1)S(1)}, bf16[128,256]{1,0:T(8,128)(2,1)}, u32[]{:S(2)}) copy-start(bf16[128,256]{1,0:T(8,128)(2,1)} %w_proj_hbm.1) | copy-start | bytes 196612
  2.6 0.8 copy-start.3
  3.4 0.7 copy-start.4

commit v3 on v2

--- a/solution.py
+++ b/solution.py
@@ -372,7 +372,7 @@
     return pl.pallas_call(
         body,
         out_shape=jax.ShapeDtypeStruct(pair.shape, F32),
-        in_specs=[pl.BlockSpec(memory_space=pl.ANY)] * 5,
+        in_specs=[pl.BlockSpec(memory_space=pltpu.HBM)] * 5,
         out_specs=pl.BlockSpec(memory_space=pltpu.VMEM),
         scratch_shapes=[
             *(pltpu.VMEM(a.shape, a.dtype) for a in args),
@@ -409,7 +409,7 @@
             pltpu.SemaphoreType.DMA((8,)),
         ],
         compiler_params=pltpu.CompilerParams(
-            collective_id=0, has_side_effects=True, vmem_limit_bytes=48 * 1024 * 1024
+            collective_id=0, has_side_effects=True, vmem_limit_bytes=60 * 1024 * 1024
         ),
     )(*args)
 

time: 83.5 us -> 80.5 us (0.964)
  local copies, waits for them, and re-layouts: 4.74 us -> 1.58 us
    unnamed x11 -> x1, local copies, waits for them, and re-layouts: 4.74 us -> 1.58 us
where the time goes in v3:
time: 80.5 us; the launch traced here: 80.2 us
  Pallas kernels  78.6 us (98%)
  local copies, waits for them, and re-layouts  1.58 us (2%)
    pallas_call x1, Pallas kernels, per_device(): pl.pallas_call(body, out_shape=jax.ShapeDtypeStruct(pair.shape, F32), in_...  78.6 us

profile of v3, /device:TPU:1, one launch (start us, length us, event | category | flops | bytes accessed | tf_op | source)
XLA Modules:
  0.0 80.2 jit_solution(18000205872470186964)
XLA Ops:
  0.0 78.6 %shard_map.55 = f32[12,24,128]{2,1,0:T(8,128)} custom-call(bf16[12,24,128]{2,1,0:T(8,128)(2,1)} %pair_hbm.1, bf16[12,24,128]{2,1,0:T(8,128)(2,1)} %d_out_hbm.1, bf16[128,256]{1,0:T(8,128)(2,1)} %w_proj_hbm.1, bf16[128,128]{1,0:T(8,128)(2,1)} %w_gate_hbm.1, bf16[64,128]{1,0:T(8,128)(2,1)} %ow_hbm.1), custom_call_target="tpu_custom_call" | custom-call | tf_op jit(solution)/shard_map/pallas_call | solution.py:372
  78.6 1.6 %copy.7 = f32[12,24,128]{2,1,0:T(8,128)} copy(f32[12,24,128]{2,1,0:T(8,128)} %shard_map.55) | data formatting | bytes 294912

commit v4 on v0

v4 whole, which is shorter than its diff:
```python
import jax
import jax.numpy as jnp
from jax import lax
from jax.experimental import pallas as pl
from jax.experimental.pallas import tpu as pltpu
from jax.sharding import PartitionSpec as P

EPS = 1e-05
MESH = pl.DeviceIdType.MESH
F32 = jnp.float32
BF16 = jnp.bfloat16

LANES = 128
GROUP = 64
PEERS = 8
HALF = 12
TILE_I = 12
CELLS = 384
TILES = CELLS // LANES


def dot(a, b):
    return lax.dot_general(a, b, (((1,), (0,)), ((), ())), preferred_element_type=F32)


def dot_t(a, b):
    return lax.dot_general(a, b, (((1,), (1,)), ((), ())), preferred_element_type=F32)


def swap_blocks(parts):
    lane = lax.broadcasted_iota(jnp.int32, parts[0].shape, 1)
    low = lane < 64
    even = (lane // 32) % 2 == 0
    p0, p1, p2, p3 = parts
    t0 = jnp.where(low, p0, pltpu.roll(p2, 64, 1))
    t2 = jnp.where(low, pltpu.roll(p0, 64, 1), p2)
    t1 = jnp.where(low, p1, pltpu.roll(p3, 64, 1))
    t3 = jnp.where(low, pltpu.roll(p1, 64, 1), p3)
    u0 = jnp.where(even, t0, pltpu.roll(t1, 32, 1))
    u1 = jnp.where(even, pltpu.roll(t0, 96, 1), t1)
    u2 = jnp.where(even, t2, pltpu.roll(t3, 32, 1))
    u3 = jnp.where(even, pltpu.roll(t2, 96, 1), t3)
    return u0, u1, u2, u3


def close_gaps(tiles):
    place = lax.broadcasted_iota(jnp.int32, tiles[0].shape, 1) % 16
    return [
        jnp.where(place < HALF, tiles[t], pltpu.roll(tiles[3], HALF - 4 * t, 1)) for t in range(3)
    ]


def open_gaps(tiles):
    place = lax.broadcasted_iota(jnp.int32, tiles[0].shape, 1) % 16
    back = [pltpu.roll(tiles[t], LANES - HALF + 4 * t, 1) for t in range(3)]
    return list(tiles) + [jnp.where(place < 4, back[0], jnp.where(place < 8, back[1], back[2]))]


def body(
    pair_hbm, d_out_hbm, w_proj_hbm, w_gate_hbm, ow_hbm, out_ref,
    pair_ref, d_out_ref, w_proj_ref, w_gate_ref, ow_ref,
    pad_ref, slots8_ref, slots4_ref, rows8_ref, rows4_ref,
    send_a, recv_a, recv_l, recv_r, send_d, recv_d, send_e, recv_e, send_f, recv_f, send_h, recv_h,
    in_sem, send_sem, recv_sem,
):
    r = lax.axis_index("row")
    c = lax.axis_index("col")
    peer = lax.rem(r, PEERS)
    x_me = lax.rem(c, 4)
    z_lo = r // PEERS
    z_me = (c // 4) * 4 + z_lo
    slot = (c // 4) * 16 + x_me * 4 + z_lo
    barrier = pltpu.get_barrier_semaphore()

    loads = [
        pltpu.make_async_copy(src, dst, in_sem.at[n])
        for n, (src, dst) in enumerate((
            (pair_hbm, pair_ref), (w_proj_hbm, w_proj_ref), (d_out_hbm, d_out_ref),
            (w_gate_hbm, w_gate_ref), (ow_hbm, ow_ref),
        ))
    ]
    for load in loads:
        load.start()

    def each_of_group(act):
        def at(dz, dx):
            z = lax.rem(z_me + dz, 16)
            x = lax.rem(x_me + dx, 4)
            act((lax.rem(z, 4) * PEERS + peer, (z // 4) * 4 + x), (z // 4) * 16 + x * 4 + lax.rem(z, 4))

        def step(n, carry):
            away = (n + 1) // 2
            dz = 8 + jnp.where(lax.rem(n, 2) == 1, away, -away)
            for dx in (2, 1, 3, 0):
                at(dz, dx)
            return carry

        lax.fori_loop(0, 15, step, 0)
        for dx in (2, 1, 3):
            at(0, dx)

    def each_peer(act):
        def step(d, carry):
            to = lax.rem(peer + d, PEERS)
            act((z_lo * PEERS + to, c), to)
            return carry

        lax.fori_loop(1, PEERS, step, 0)

    def greet(device, _):
        pl.semaphore_signal(barrier, inc=1, device_id=device, device_id_type=MESH)

    each_of_group(greet)
    each_peer(greet)

    def wait_all(ref, sem):
        pltpu.make_async_copy(ref, ref, sem).wait()

    def exchange(phase, send, recv):
        def one(device, to):
            pltpu.make_async_remote_copy(
                src_ref=send.at[to], dst_ref=recv.at[slot],
                send_sem=send_sem.at[phase], recv_sem=recv_sem.at[phase],
                device_id=device, device_id_type=MESH,
            ).start()

        each_of_group(one)
        pltpu.make_async_copy(send.at[slot], recv.at[slot], recv_sem.at[phase]).start()

    def share(phase, src_of, recv):
        def one(device, to):
            pltpu.make_async_remote_copy(
                src_ref=src_of(to), dst_ref=recv.at[peer],
                send_sem=send_sem.at[phase], recv_sem=recv_sem.at[phase],
                device_id=device, device_id_type=MESH,
            ).start()

        each_peer(one)

    def wait_sends(phase, ref):
        wait_all(ref.at[pl.ds(0, ref.shape[0] - 1)], send_sem.at[phase])

    def padded_transpose(ref):
        for i in range(TILE_I):
            cells = ref[i].astype(F32)
            pad_ref[32 * i : 32 * i + HALF, :] = cells[:HALF]
            pad_ref[32 * i + 16 : 32 * i + 16 + HALF, :] = cells[HALF:]
        return pad_ref[...].T

    def tile_of(array, t):
        return array[:, LANES * t : LANES * (t + 1)]

    pad_ref[...] = jnp.zeros_like(pad_ref)
    slots8_ref[...] = jnp.zeros_like(slots8_ref)
    slots4_ref[...] = jnp.zeros_like(slots4_ref)
    new = lax.broadcasted_iota(jnp.int32, (256, 256), 0)
    old = lax.broadcasted_iota(jnp.int32, (256, 256), 1)
    order = (old == (new % 2) * 128 + (new // 128) * 64 + (new // 2) % 64).astype(F32).astype(BF16)
    eye = (
        lax.broadcasted_iota(jnp.int32, (128, 128), 0) == lax.broadcasted_iota(jnp.int32, (128, 128), 1)
    ).astype(F32).astype(BF16)

    loads[0].wait()
    values = padded_transpose(pair_ref)
    centre = values - jnp.mean(values, axis=0, keepdims=True)
    inv_std = lax.rsqrt(jnp.mean(centre * centre, axis=0, keepdims=True) + EPS)
    zhat = centre * inv_std
    normed = zhat.astype(BF16)
    loads[1].wait()
    w_rows = dot_t(order, w_proj_ref[...]).astype(BF16)
    projected = dot(w_rows, normed)
    gates = jax.nn.sigmoid(projected[:128])
    vals = projected[128:]
    left_right = gates * vals
    for a in range(TILES):
        slots8_ref[pl.ds(a, 128, stride=4), :] = tile_of(left_right, a)
    send_a[...] = slots8_ref[...].astype(BF16).reshape(GROUP, 8, LANES)

    pl.semaphore_wait(barrier, GROUP - 1 + PEERS - 1)
    exchange(0, send_a, recv_a)

    for load in loads[2:]:
        load.wait()
    w_cols = dot_t(w_proj_ref[...], order).astype(BF16)
    w_gate_t = dot_t(eye, w_gate_ref[...]).astype(BF16)
    ow_t = dot_t(eye, ow_ref[...]).astype(BF16)
    upstream = padded_transpose(d_out_ref)
    gate = jax.nn.sigmoid(dot(w_gate_t, normed))
    d_xhat = dot(ow_ref[...], (upstream * gate).astype(BF16))
    d_xhat_mean = jnp.mean(d_xhat, axis=0, keepdims=True)
    gate_slope = upstream * gate * (1.0 - gate)

    wait_all(recv_a, recv_sem.at[0])
    for zh in range(4):
        for zl in range(4):
            parts = [recv_a[16 * zh + 4 * x + zl].astype(F32) for x in range(4)]
            for b, part in enumerate(swap_blocks(parts)):
                rows8_ref[zh, pl.ds(32 * zl + b, 8, stride=4), :] = part
    for t, tile in enumerate(close_gaps([rows8_ref[zh] for zh in range(4)])):
        both = tile.astype(BF16).reshape(4, 2, 16, LANES)
        recv_l[peer, :, t] = both[:, 0]
        recv_r[peer, :, t] = both[:, 1]
    share(1, lambda to: recv_r.at[peer], recv_r)
    share(2, lambda to: recv_l.at[peer], recv_l)

    def own_rows(ref):
        return jnp.concatenate([ref[peer, :, t].reshape(64, LANES) for t in range(TILES)], axis=1)

    def all_rows(ref):
        return jnp.concatenate(
            [
                jnp.concatenate([ref[:, zl, t].reshape(128, LANES) for zl in range(4)], axis=0)
                for t in range(TILES)
            ],
            axis=1,
        )

    wait_sends(0, send_a)
    wait_all(recv_r.at[pl.ds(0, PEERS - 1)], recv_sem.at[1])
    right = all_rows(recv_r)
    x_rows = dot_t(own_rows(recv_l), right)
    for zh in range(4):
        rows4_ref[zh] = tile_of(x_rows, zh)
    for zh in range(4):
        for pair in range(2):
            parts = [rows4_ref[zh, pl.ds(32 * pair + b, 8, stride=4), :] for b in range(4)]
            for x, part in enumerate(swap_blocks(parts)):
                first = 16 * zh + 4 * x + 2 * pair
                send_d[first] = part[:4].astype(BF16)
                send_d[first + 1] = part[4:].astype(BF16)
    exchange(3, send_d, recv_d)
    wait_sends(1, recv_r)
    wait_all(recv_d, recv_sem.at[3])

    for n in range(GROUP):
        slots4_ref[4 * n : 4 * n + 4, :] = recv_d[n].astype(F32)
    x = jnp.concatenate([slots4_ref[pl.ds(a, GROUP, stride=4), :] for a in range(TILES)], axis=1)
    x_centre = x - jnp.mean(x, axis=0, keepdims=True)
    x_inv = lax.rsqrt(jnp.mean(x_centre * x_centre, axis=0, keepdims=True) + EPS)
    xhat = x_centre * x_inv
    d_x = (d_xhat - d_xhat_mean - xhat * jnp.mean(d_xhat * xhat, axis=0, keepdims=True)) * x_inv
    slots4_ref[...] = jnp.zeros_like(slots4_ref)
    for a in range(TILES):
        slots4_ref[pl.ds(a, GROUP, stride=4), :] = tile_of(d_x, a)
    for n in range(GROUP):
        send_e[n] = slots4_ref[4 * n : 4 * n + 4, :].astype(BF16)
    exchange(4, send_e, recv_e)

    mixed = dot(ow_t, xhat.astype(BF16))
    d_gate = (mixed * gate_slope).astype(BF16)
    d_normed_gate = dot(w_gate_ref[...], d_gate)
    wait_sends(2, recv_l)
    wait_sends(3, send_d)

    wait_all(recv_e, recv_sem.at[4])
    for zh in range(4):
        for pair in range(2):
            parts = []
            for x in range(4):
                first = 16 * zh + 4 * x + 2 * pair
                parts.append(jnp.concatenate([recv_e[first].astype(F32), recv_e[first + 1].astype(F32)], axis=0))
            for b, part in enumerate(swap_blocks(parts)):
                rows4_ref[zh, pl.ds(32 * pair + b, 8, stride=4), :] = part
    d_x_rows = jnp.concatenate([rows4_ref[zh] for zh in range(4)], axis=1)
    d_x_cols = jnp.concatenate([d_x_rows, jnp.zeros_like(d_x_rows)], axis=0).T.astype(BF16)
    d_x_cols = d_x_cols.reshape(4, PEERS, 16, LANES)
    for to in range(PEERS):
        send_f[to] = d_x_cols[:, to]
    recv_f[peer] = send_f[peer]
    share(5, lambda to: send_f.at[to], recv_f)

    d_left = dot(d_x_rows.astype(BF16), right)
    for zh, tile in enumerate(open_gaps([tile_of(d_left, t) for t in range(TILES)])):
        for zl in range(4):
            rows8_ref[zh, 32 * zl : 32 * zl + 16, :] = tile[16 * zl : 16 * zl + 16]
    wait_sends(4, send_e)
    wait_all(recv_l.at[pl.ds(0, PEERS - 1)], recv_sem.at[2])
    wait_all(recv_f.at[pl.ds(0, PEERS - 1)], recv_sem.at[5])
    d_right = None
    for g in range(PEERS):
        left_g = jnp.concatenate([recv_l[g, :, t].reshape(64, LANES) for t in range(TILES)], axis=1)
        term = dot(recv_f[g].reshape(64, LANES)[:, :64], left_g)
        d_right = term if d_right is None else d_right + term
    for zh, tile in enumerate(open_gaps([tile_of(d_right, t) for t in range(TILES)])):
        for zl in range(4):
            rows8_ref[zh, 32 * zl + 16 : 32 * zl + 32, :] = tile[16 * zl : 16 * zl + 16]
    for zh in range(4):
        for zl in range(4):
            parts = [rows8_ref[zh, pl.ds(32 * zl + b, 8, stride=4), :] for b in range(4)]
            for x, part in enumerate(swap_blocks(parts)):
                send_h[16 * zh + 4 * x + zl] = part.astype(BF16)
    exchange(6, send_h, recv_h)
    wait_sends(5, send_f)
    wait_all(recv_h, recv_sem.at[6])

    slots8_ref[...] = recv_h[...].astype(F32).reshape(GROUP * 8, LANES)
    d_lr = jnp.concatenate([slots8_ref[pl.ds(a, 128, stride=4), :] for a in range(TILES)], axis=1)
    d_vals = d_lr * gates
    d_gates = d_vals * vals * (1.0 - gates)
    d_projected = jnp.concatenate([d_gates.astype(BF16), d_vals.astype(BF16)], axis=0)
    d_normed = dot(w_cols, d_projected) + d_normed_gate
    grad_mean = jnp.mean(d_normed, axis=0, keepdims=True)
    cross_mean = jnp.mean(d_normed * zhat, axis=0, keepdims=True)
    pad_ref[...] = ((d_normed - grad_mean - zhat * cross_mean) * inv_std).T
    for i in range(TILE_I):
        out_ref[i, :HALF, :] = pad_ref[32 * i : 32 * i + HALF, :]
        out_ref[i, HALF:, :] = pad_ref[32 * i + 16 : 32 * i + 16 + HALF, :]
    wait_sends(6, send_h)


def per_device(pair, d_out, w_proj, w_gate, output_weight):
    slots8 = pltpu.VMEM((GROUP, 8, LANES), BF16)
    slots4 = pltpu.VMEM((GROUP, 4, LANES), BF16)
    rows = pltpu.VMEM((PEERS, 4, TILES, 16, LANES), BF16)
    blocks = pltpu.VMEM((PEERS, 4, 16, LANES), BF16)
    args = (pair, d_out, w_proj, w_gate, output_weight)
    return pl.pallas_call(
        body,
        out_shape=jax.ShapeDtypeStruct(pair.shape, F32),
        in_specs=[pl.BlockSpec(memory_space=pltpu.HBM)] * 5,
        out_specs=pl.BlockSpec(memory_space=pltpu.VMEM),
        scratch_shapes=[
            *(pltpu.VMEM(a.shape, a.dtype) for a in args),
            pltpu.VMEM((CELLS, LANES), F32),
            pltpu.VMEM((GROUP * 8, LANES), F32),
            pltpu.VMEM((GROUP * 4, LANES), F32),
            pltpu.VMEM((4, 128, LANES), F32),
            pltpu.VMEM((4, 64, LANES), F32),
            slots8, slots8,
            rows, rows,
            slots4, slots4,
            slots4, slots4,
            blocks, blocks,
            slots8, slots8,
            pltpu.SemaphoreType.DMA((5,)),
            pltpu.SemaphoreType.DMA((7,)),
            pltpu.SemaphoreType.DMA((7,)),
        ],
        compiler_params=pltpu.CompilerParams(
            collective_id=0, has_side_effects=True, vmem_limit_bytes=60 * 1024 * 1024
        ),
    )(*args)


def solution(mesh):
    return jax.shard_map(
        per_device,
        mesh=mesh,
        in_specs=(P("row", "col", None), P("row", "col", None), P(), P(), P()),
        out_specs=P("row", "col", None),
        check_vma=False,
    )
```

time: 639 us -> 68.1 us (0.11)
  waiting for transfers between devices: 418 us -> 0 us
  blocking collectives: 122 us -> 0 us
  Pallas kernels: 0 us -> 65.2 us
  local copies, waits for them, and re-layouts: 41.4 us -> 1.58 us
  starting transfers between devices: 17.8 us -> 0 us
  other arithmetic: 14.1 us -> 0 us
  between operations: 13.4 us -> 0.01 us
  matrix products: 7.03 us -> 0 us
    reduce_scatter x2 -> x0, waiting for transfers between devices: 235 us -> none  [the longest x1 150 us: per_device(): lax.psum_scatter(returned, 'row', scatter_dimension=1, tiled=True)]
    all_gather x1 -> x0, blocking collectives: 122 us -> none  [per_device(): left_panel = lax.all_gather(left_tile, 'col', axis=2, tiled=True)]
    all_to_all x2 -> x0, waiting for transfers between devices: 111 us -> none  [the longest x1 111 us: per_device(): lax.all_to_all(right_terms, 'col', split_axis=2, concat_axis=1, tiled=True)]
    all_gather x1 -> x0, waiting for transfers between devices: 71.7 us -> none  [per_device(): right_columns = lax.all_gather(right_tile, 'row', axis=1, tiled=True)]
    pallas_call x0 -> x1, Pallas kernels: none -> 65.2 us  [per_device(): pl.pallas_call(body, out_shape=jax.ShapeDtypeStruct(pair.shape, F32), in_...]
    unnamed x34 -> x1, local copies, waits for them, and re-layouts: 19.2 us -> 1.58 us
    all_to_all x2 -> x0, starting transfers between devices: 17.5 us -> none  [the longest x1 13.1 us: per_device(): lax.all_to_all(right_columns, 'col', split_axis=1, concat_axis=2, tiled=T...]
    all_to_all x4 -> x0, local copies, waits for them, and re-layouts: 11 us -> none  [the longest x2 5.89 us: per_device(): lax.all_to_all(right_terms, 'col', split_axis=2, concat_axis=1, tiled=True)]
  transfers between devices with their start and end apart: 5 -> 0, of which waited for: 4 -> 0; matrix products, arithmetic and copies ran while one was open for 4% -> 0% of each run, Pallas kernels for 0% -> 0%
where the time goes in v4:
time: 68.1 us; the launch traced here: 66.8 us
  Pallas kernels  65.2 us (96%)
  local copies, waits for them, and re-layouts  1.58 us (2%)
    pallas_call x1, Pallas kernels, per_device(): pl.pallas_call(body, out_shape=jax.ShapeDtypeStruct(pair.shape, F32), in_...  65.2 us
    unnamed x1, local copies, waits for them, and re-layouts  1.58 us

profile of v4, /device:TPU:1, one launch (start us, length us, event | category | flops | bytes accessed | tf_op | source)
XLA Modules:
  0.0 66.8 jit_solution(4623481650870759518)
XLA Ops:
  0.0 65.2 %shard_map.55 = f32[12,24,128]{2,1,0:T(8,128)} custom-call(bf16[12,24,128]{2,1,0:T(8,128)(2,1)} %pair_hbm.1, bf16[12,24,128]{2,1,0:T(8,128)(2,1)} %d_out_hbm.1, bf16[128,256]{1,0:T(8,128)(2,1)} %w_proj_hbm.1, bf16[128,128]{1,0:T(8,128)(2,1)} %w_gate_hbm.1, bf16[64,128]{1,0:T(8,128)(2,1)} %ow_hbm.1), custom_call_target="tpu_custom_call" | custom-call | tf_op jit(solution)/shard_map/pallas_call | solution.py:317
  65.2 1.6 %copy.7 = f32[12,24,128]{2,1,0:T(8,128)} copy(f32[12,24,128]{2,1,0:T(8,128)} %shard_map.55) | data formatting | bytes 294912

commit v5 on v4

v5 whole, which is shorter than its diff:
```python
import jax
import jax.numpy as jnp
from jax import lax
from jax.experimental import pallas as pl
from jax.experimental.pallas import tpu as pltpu
from jax.sharding import PartitionSpec as P

EPS = 1e-05
MESH = pl.DeviceIdType.MESH
F32 = jnp.float32
BF16 = jnp.bfloat16

LANES = 128
GROUP = 64
PEERS = 8
HALF = 12
TILE_I = 12
CELLS = 384
TILES = CELLS // LANES


def dot(a, b):
    return lax.dot_general(a, b, (((1,), (0,)), ((), ())), preferred_element_type=F32)


def dot_t(a, b):
    return lax.dot_general(a, b, (((1,), (1,)), ((), ())), preferred_element_type=F32)


def swap_blocks(parts):
    lane = lax.broadcasted_iota(jnp.int32, parts[0].shape, 1)
    low = lane < 64
    even = (lane // 32) % 2 == 0
    p0, p1, p2, p3 = parts
    t0 = jnp.where(low, p0, pltpu.roll(p2, 64, 1))
    t2 = jnp.where(low, pltpu.roll(p0, 64, 1), p2)
    t1 = jnp.where(low, p1, pltpu.roll(p3, 64, 1))
    t3 = jnp.where(low, pltpu.roll(p1, 64, 1), p3)
    u0 = jnp.where(even, t0, pltpu.roll(t1, 32, 1))
    u1 = jnp.where(even, pltpu.roll(t0, 96, 1), t1)
    u2 = jnp.where(even, t2, pltpu.roll(t3, 32, 1))
    u3 = jnp.where(even, pltpu.roll(t2, 96, 1), t3)
    return u0, u1, u2, u3


def close_gaps(tiles):
    place = lax.broadcasted_iota(jnp.int32, tiles[0].shape, 1) % 16
    return [
        jnp.where(place < HALF, tiles[t], pltpu.roll(tiles[3], HALF - 4 * t, 1)) for t in range(3)
    ]


def open_gaps(tiles):
    place = lax.broadcasted_iota(jnp.int32, tiles[0].shape, 1) % 16
    back = [pltpu.roll(tiles[t], LANES - HALF + 4 * t, 1) for t in range(3)]
    return list(tiles) + [jnp.where(place < 4, back[0], jnp.where(place < 8, back[1], back[2]))]


def body(
    pair_hbm, d_out_hbm, w_proj_hbm, w_gate_hbm, ow_hbm, out_ref,
    pair_ref, d_out_ref, w_proj_ref, w_gate_ref, ow_ref,
    pad_ref, slots_ref, rows_ref, left_ref, right_ref,
    send_a, recv_a, send_b, recv_b, send_d, recv_d, send_e, recv_e, send_f, recv_f, send_g, recv_g, send_h, recv_h,
    in_sem, send_sem, recv_sem,
):
    r = lax.axis_index("row")
    c = lax.axis_index("col")
    peer = lax.rem(r, PEERS)
    x_me = lax.rem(c, 4)
    z_lo = r // PEERS
    z_me = (c // 4) * 4 + z_lo
    slot = (c // 4) * 16 + x_me * 4 + z_lo
    barrier = pltpu.get_barrier_semaphore()

    def each_of_group(act):
        def at(dz, dx):
            z = lax.rem(z_me + dz, 16)
            x = lax.rem(x_me + dx, 4)
            act((lax.rem(z, 4) * PEERS + peer, (z // 4) * 4 + x), (z // 4) * 16 + x * 4 + lax.rem(z, 4))

        def step(n, carry):
            away = (n + 1) // 2
            dz = 8 + jnp.where(lax.rem(n, 2) == 1, away, -away)
            for dx in (2, 1, 3, 0):
                at(dz, dx)
            return carry

        lax.fori_loop(0, 15, step, 0)
        for dx in (2, 1, 3):
            at(0, dx)

    def each_peer(act):
        def step(d, carry):
            to = lax.rem(peer + d, PEERS)
            act((z_lo * PEERS + to, c), to)
            return carry

        lax.fori_loop(1, PEERS, step, 0)

    def greet(device, _):
        pl.semaphore_signal(barrier, inc=1, device_id=device, device_id_type=MESH)

    each_of_group(greet)
    each_peer(greet)

    loads = [
        pltpu.make_async_copy(src, dst, in_sem.at[n])
        for n, (src, dst) in enumerate((
            (pair_hbm, pair_ref), (w_proj_hbm, w_proj_ref), (d_out_hbm, d_out_ref),
            (w_gate_hbm, w_gate_ref), (ow_hbm, ow_ref),
        ))
    ]
    for load in loads:
        load.start()

    def wait_all(ref, sem):
        pltpu.make_async_copy(ref, ref, sem).wait()

    def exchange(phase, send, recv):
        def one(device, to):
            pltpu.make_async_remote_copy(
                src_ref=send.at[to], dst_ref=recv.at[slot],
                send_sem=send_sem.at[phase], recv_sem=recv_sem.at[phase],
                device_id=device, device_id_type=MESH,
            ).start()

        each_of_group(one)
        pltpu.make_async_copy(send.at[slot], recv.at[slot], recv_sem.at[phase]).start()

    def share(phase, src_of, recv):
        def one(device, to):
            pltpu.make_async_remote_copy(
                src_ref=src_of(to), dst_ref=recv.at[peer],
                send_sem=send_sem.at[phase], recv_sem=recv_sem.at[phase],
                device_id=device, device_id_type=MESH,
            ).start()

        each_peer(one)

    def wait_sends(phase, ref):
        wait_all(ref.at[pl.ds(0, ref.shape[0] - 1)], send_sem.at[phase])

    def padded_transpose(ref):
        for i in range(TILE_I):
            cells = ref[i].astype(F32)
            pad_ref[32 * i : 32 * i + HALF, :] = cells[:HALF]
            pad_ref[32 * i + 16 : 32 * i + 16 + HALF, :] = cells[HALF:]
        return pad_ref[...].T

    def tile_of(array, t):
        return array[:, LANES * t : LANES * (t + 1)]

    def to_slots(array, send):
        for a in range(TILES):
            slots_ref[pl.ds(a, GROUP, stride=4), :] = tile_of(array, a)
        for n in range(GROUP):
            send[n] = slots_ref[4 * n : 4 * n + 4, :].astype(BF16)

    def from_slots(recv):
        for n in range(GROUP):
            slots_ref[4 * n : 4 * n + 4, :] = recv[n].astype(F32)
        return jnp.concatenate([slots_ref[pl.ds(a, GROUP, stride=4), :] for a in range(TILES)], axis=1)

    def gather_rows(recv):
        for zh in range(4):
            for pair in range(2):
                parts = []
                for x in range(4):
                    first = 16 * zh + 4 * x + 2 * pair
                    parts.append(jnp.concatenate([recv[first].astype(F32), recv[first + 1].astype(F32)], axis=0))
                for b, part in enumerate(swap_blocks(parts)):
                    rows_ref[zh, pl.ds(32 * pair + b, 8, stride=4), :] = part
            for zl in range(3):
                rows_ref[zh, 16 * zl + HALF : 16 * zl + 16, :] = rows_ref[zh, 48 + 4 * zl : 52 + 4 * zl, :]
        return close_gaps([rows_ref[zh, :48, :] for zh in range(4)])

    def scatter_rows(array, send):
        for zh, tile in enumerate(open_gaps([tile_of(array, t) for t in range(TILES)])):
            rows_ref[zh, :48, :] = tile
            for zl in range(3):
                rows_ref[zh, 48 + 4 * zl : 52 + 4 * zl, :] = rows_ref[zh, 16 * zl + HALF : 16 * zl + 16, :]
            for pair in range(2):
                parts = [rows_ref[zh, pl.ds(32 * pair + b, 8, stride=4), :] for b in range(4)]
                for x, part in enumerate(swap_blocks(parts)):
                    first = 16 * zh + 4 * x + 2 * pair
                    send[first] = part[:4].astype(BF16)
                    send[first + 1] = part[4:].astype(BF16)

    def rows_of(ref, g):
        return jnp.concatenate([ref[g, :, t].reshape(48, LANES) for t in range(TILES)], axis=1)

    def all_rows(ref):
        return jnp.concatenate(
            [
                jnp.concatenate([ref[:, zl, t].reshape(128, LANES) for zl in range(3)], axis=0)
                for t in range(TILES)
            ],
            axis=1,
        )

    pad_ref[...] = jnp.zeros_like(pad_ref)
    slots_ref[...] = jnp.zeros_like(slots_ref)
    loads[0].wait()
    values = padded_transpose(pair_ref)
    centre = values - jnp.mean(values, axis=0, keepdims=True)
    inv_std = lax.rsqrt(jnp.mean(centre * centre, axis=0, keepdims=True) + EPS)
    zhat = centre * inv_std
    normed = zhat.astype(BF16)
    loads[1].wait()
    w_rows = w_proj_ref[...].astype(F32).T.astype(BF16)
    projected = dot(w_rows[128:], normed)
    right_gate = jax.nn.sigmoid(projected[:64])
    right_value = projected[64:]
    to_slots(right_gate * right_value, send_a)

    pl.semaphore_wait(barrier, GROUP - 1 + PEERS - 1)
    exchange(0, send_a, recv_a)

    projected = dot(w_rows[:128], normed)
    left_gate = jax.nn.sigmoid(projected[:64])
    left_value = projected[64:]
    to_slots(left_gate * left_value, send_b)
    exchange(1, send_b, recv_b)

    for load in loads[2:]:
        load.wait()
    w_gate_t = w_gate_ref[...].astype(F32).T.astype(BF16)
    ow_t = ow_ref[...].astype(F32).T.astype(BF16)
    upstream = padded_transpose(d_out_ref)
    gate = jax.nn.sigmoid(dot(w_gate_t, normed))
    d_xhat = dot(ow_ref[...], (upstream * gate).astype(BF16))
    d_xhat_mean = jnp.mean(d_xhat, axis=0, keepdims=True)
    gate_slope = upstream * gate * (1.0 - gate)

    wait_all(recv_a, recv_sem.at[0])
    for t, tile in enumerate(gather_rows(recv_a)):
        right_ref[peer, :, t] = tile.astype(BF16).reshape(3, 16, LANES)
    share(2, lambda to: right_ref.at[peer], right_ref)
    wait_all(recv_b, recv_sem.at[1])
    for t, tile in enumerate(gather_rows(recv_b)):
        left_ref[peer, :, t] = tile.astype(BF16).reshape(3, 16, LANES)
    share(3, lambda to: left_ref.at[peer], left_ref)
    wait_sends(0, send_a)
    wait_sends(1, send_b)
    wait_all(right_ref.at[pl.ds(0, PEERS - 1)], recv_sem.at[2])
    right = all_rows(right_ref)
    scatter_rows(dot_t(rows_of(left_ref, peer), right), send_d)
    exchange(4, send_d, recv_d)
    wait_sends(2, right_ref)
    wait_all(recv_d, recv_sem.at[4])

    x = from_slots(recv_d)
    x_centre = x - jnp.mean(x, axis=0, keepdims=True)
    x_inv = lax.rsqrt(jnp.mean(x_centre * x_centre, axis=0, keepdims=True) + EPS)
    xhat = x_centre * x_inv
    d_x = (d_xhat - d_xhat_mean - xhat * jnp.mean(d_xhat * xhat, axis=0, keepdims=True)) * x_inv
    slots_ref[...] = jnp.zeros_like(slots_ref)
    to_slots(d_x, send_e)
    exchange(5, send_e, recv_e)

    mixed = dot(ow_t, xhat.astype(BF16))
    d_gate = (mixed * gate_slope).astype(BF16)
    d_normed = dot(w_gate_ref[...], d_gate)
    wait_sends(3, left_ref)
    wait_sends(4, send_d)

    wait_all(recv_e, recv_sem.at[5])
    d_x_rows = jnp.concatenate(gather_rows(recv_e), axis=1)
    padded = jnp.concatenate([d_x_rows, jnp.zeros((80, CELLS), F32)], axis=0)
    d_x_cols = padded.T.astype(BF16).reshape(3, PEERS, 16, LANES)
    for to in range(PEERS):
        send_f[to] = d_x_cols[:, to]
    recv_f[peer] = send_f[peer]
    share(6, lambda to: send_f.at[to], recv_f)

    scatter_rows(dot(d_x_rows.astype(BF16), right), send_g)
    exchange(7, send_g, recv_g)
    wait_sends(5, send_e)
    wait_all(left_ref.at[pl.ds(0, PEERS - 1)], recv_sem.at[3])
    wait_all(recv_f.at[pl.ds(0, PEERS - 1)], recv_sem.at[6])
    d_right = None
    for g in range(PEERS):
        term = dot(recv_f[g].reshape(48, LANES)[:, :48], rows_of(left_ref, g))
        d_right = term if d_right is None else d_right + term
    scatter_rows(d_right, send_h)
    exchange(8, send_h, recv_h)

    def back(grad, gates, vals, columns):
        d_vals = grad * gates
        d_gates = d_vals * vals * (1.0 - gates)
        return dot(columns, jnp.concatenate([d_gates.astype(BF16), d_vals.astype(BF16)], axis=0))

    wait_sends(6, send_f)
    wait_all(recv_g, recv_sem.at[7])
    d_normed += back(from_slots(recv_g), left_gate, left_value, w_proj_ref[:, :128])
    wait_sends(7, send_g)
    wait_all(recv_h, recv_sem.at[8])
    d_normed += back(from_slots(recv_h), right_gate, right_value, w_proj_ref[:, 128:])
    grad_mean = jnp.mean(d_normed, axis=0, keepdims=True)
    cross_mean = jnp.mean(d_normed * zhat, axis=0, keepdims=True)
    pad_ref[...] = ((d_normed - grad_mean - zhat * cross_mean) * inv_std).T
    for i in range(TILE_I):
        out_ref[i, :HALF, :] = pad_ref[32 * i : 32 * i + HALF, :]
        out_ref[i, HALF:, :] = pad_ref[32 * i + 16 : 32 * i + 16 + HALF, :]
    wait_sends(8, send_h)


def per_device(pair, d_out, w_proj, w_gate, output_weight):
    slots = pltpu.VMEM((GROUP, 4, LANES), BF16)
    rows = pltpu.VMEM((PEERS, 3, TILES, 16, LANES), BF16)
    blocks = pltpu.VMEM((PEERS, 3, 16, LANES), BF16)
    args = (pair, d_out, w_proj, w_gate, output_weight)
    return pl.pallas_call(
        body,
        out_shape=jax.ShapeDtypeStruct(pair.shape, F32),
        in_specs=[pl.BlockSpec(memory_space=pltpu.HBM)] * 5,
        out_specs=pl.BlockSpec(memory_space=pltpu.VMEM),
        scratch_shapes=[
            *(pltpu.VMEM(a.shape, a.dtype) for a in args),
            pltpu.VMEM((CELLS, LANES), F32),
            pltpu.VMEM((GROUP * 4, LANES), F32),
            pltpu.VMEM((4, 64, LANES), F32),
            rows, rows,
            slots, slots,
            slots, slots,
            slots, slots,
            slots, slots,
            blocks, blocks,
            slots, slots,
            slots, slots,
            pltpu.SemaphoreType.DMA((5,)),
            pltpu.SemaphoreType.DMA((9,)),
            pltpu.SemaphoreType.DMA((9,)),
        ],
        compiler_params=pltpu.CompilerParams(
            collective_id=0, has_side_effects=True, vmem_limit_bytes=60 * 1024 * 1024
        ),
    )(*args)


def solution(mesh):
    return jax.shard_map(
        per_device,
        mesh=mesh,
        in_specs=(P("row", "col", None), P("row", "col", None), P(), P(), P()),
        out_specs=P("row", "col", None),
        check_vma=False,
    )
```

time: 68.1 us -> 65.7 us (0.965); the launches traced: 66.8 us -> 65.6 us
  Pallas kernels: 65.2 us -> 64 us
    pallas_call x1, Pallas kernels: 65.2 us -> 64 us  [per_device(): pl.pallas_call(body, out_shape=jax.ShapeDtypeStruct(pair.shape, F32), in_...]
where the time goes in v5:
time: 65.7 us; the launch traced here: 65.6 us
  Pallas kernels  64 us (97%)
  local copies, waits for them, and re-layouts  1.58 us (2%)
    pallas_call x1, Pallas kernels, per_device(): pl.pallas_call(body, out_shape=jax.ShapeDtypeStruct(pair.shape, F32), in_...  64 us
    unnamed x1, local copies, waits for them, and re-layouts  1.58 us

profile of v5, /device:TPU:1, one launch (start us, length us, event | category | flops | bytes accessed | tf_op | source)
XLA Modules:
  0.0 65.6 jit_solution(12398795329414595161)
XLA Ops:
  0.0 64.0 %shard_map.55 = f32[12,24,128]{2,1,0:T(8,128)} custom-call(bf16[12,24,128]{2,1,0:T(8,128)(2,1)} %pair_hbm.1, bf16[12,24,128]{2,1,0:T(8,128)(2,1)} %d_out_hbm.1, bf16[128,256]{1,0:T(8,128)(2,1)} %w_proj_hbm.1, bf16[128,128]{1,0:T(8,128)(2,1)} %w_gate_hbm.1, bf16[64,128]{1,0:T(8,128)(2,1)} %ow_hbm.1), custom_call_target="tpu_custom_call" | custom-call | tf_op jit(solution)/shard_map/pallas_call | solution.py:313
  64.0 1.6 %copy.7 = f32[12,24,128]{2,1,0:T(8,128)} copy(f32[12,24,128]{2,1,0:T(8,128)} %shard_map.55) | data formatting | bytes 294912

commit v6 on v5

--- a/solution.py
+++ b/solution.py
@@ -61,7 +61,7 @@
     pair_ref, d_out_ref, w_proj_ref, w_gate_ref, ow_ref,
     pad_ref, slots_ref, rows_ref, left_ref, right_ref,
     send_a, recv_a, send_b, recv_b, send_d, recv_d, send_e, recv_e, send_f, recv_f, send_g, recv_g, send_h, recv_h,
-    in_sem, send_sem, recv_sem,
+    in_sem, send_sem, recv_sem, across_sem,
 ):
     r = lax.axis_index("row")
     c = lax.axis_index("col")
@@ -136,6 +136,25 @@
             ).start()
 
         each_peer(one)
+
+    def move_right(block, to, send, recv):
+        pltpu.make_async_remote_copy(
+            src_ref=right_ref.at[block], dst_ref=right_ref.at[block], send_sem=send, recv_sem=recv,
+            device_id=(z_lo * PEERS + to, c), device_id_type=MESH,
+        ).start()
+
+    sibling = peer + 1 - 2 * lax.rem(peer, 2)
+
+    def start_across():
+        for d in (2, 1, 3):
+            move_right(peer, lax.rem(peer + 2 * d, PEERS), send_sem.at[2], across_sem.at[d])
+        move_right(peer, sibling, send_sem.at[9], recv_sem.at[2])
+
+    def to_sibling():
+        for d in (1, 3, 2):
+            block = lax.rem(peer + PEERS - 2 * d, PEERS)
+            wait_all(right_ref.at[block], across_sem.at[d])
+            move_right(block, sibling, send_sem.at[9], recv_sem.at[2])
 
     def wait_sends(phase, ref):
         wait_all(ref.at[pl.ds(0, ref.shape[0] - 1)], send_sem.at[phase])
@@ -235,18 +254,20 @@
     wait_all(recv_a, recv_sem.at[0])
     for t, tile in enumerate(gather_rows(recv_a)):
         right_ref[peer, :, t] = tile.astype(BF16).reshape(3, 16, LANES)
-    share(2, lambda to: right_ref.at[peer], right_ref)
+    start_across()
     wait_all(recv_b, recv_sem.at[1])
     for t, tile in enumerate(gather_rows(recv_b)):
         left_ref[peer, :, t] = tile.astype(BF16).reshape(3, 16, LANES)
-    share(3, lambda to: left_ref.at[peer], left_ref)
+    to_sibling()
     wait_sends(0, send_a)
     wait_sends(1, send_b)
-    wait_all(right_ref.at[pl.ds(0, PEERS - 1)], recv_sem.at[2])
+    wait_all(right_ref.at[pl.ds(0, 4)], recv_sem.at[2])
     right = all_rows(right_ref)
     scatter_rows(dot_t(rows_of(left_ref, peer), right), send_d)
     exchange(4, send_d, recv_d)
-    wait_sends(2, right_ref)
+    share(3, lambda to: left_ref.at[peer], left_ref)
+    wait_all(right_ref.at[pl.ds(0, 3)], send_sem.at[2])
+    wait_all(right_ref.at[pl.ds(0, 4)], send_sem.at[9])
     wait_all(recv_d, recv_sem.at[4])
 
     x = from_slots(recv_d)
@@ -329,13 +350,14 @@
             slots, slots,
             slots, slots,
             pltpu.SemaphoreType.DMA((5,)),
+            pltpu.SemaphoreType.DMA((10,)),
             pltpu.SemaphoreType.DMA((9,)),
-            pltpu.SemaphoreType.DMA((9,)),
+            pltpu.SemaphoreType.DMA((4,)),
         ],
         compiler_params=pltpu.CompilerParams(
-            collective_id=0, has_side_effects=True, vmem_limit_bytes=60 * 1024 * 1024
+            collective_id=0, has_side_effects=True, vmem_limit_bytes=48 * 1024 * 1024
         ),
-    )(*args)
+    )(*(pltpu.with_memory_space_constraint(a, pltpu.HBM) for a in args))
 
 
 def solution(mesh):

time: 65.7 us -> 62.1 us (0.945)
  Pallas kernels: 64 us -> 61.2 us
  local copies, waits for them, and re-layouts: 1.58 us -> 0.66 us
    pallas_call x1, Pallas kernels: 64 us -> 61.2 us  [per_device(): pl.pallas_call(body, out_shape=jax.ShapeDtypeStruct(pair.shape, F32), in_...]
    unnamed x1, local copies, waits for them, and re-layouts: 1.58 us -> 0.66 us
where the time goes in v6:
time: 62.1 us; the launch traced here: 61.9 us
  Pallas kernels  61.2 us (99%)
  local copies, waits for them, and re-layouts  0.66 us (1%)
    pallas_call x1, Pallas kernels, per_device(): pl.pallas_call(body, out_shape=jax.ShapeDtypeStruct(pair.shape, F32), in_...  61.2 us

profile of v6, /device:TPU:1, one launch (start us, length us, event | category | flops | bytes accessed | tf_op | source)
XLA Modules:
  0.0 61.9 jit_solution(10572191952328481710)
XLA Ops:
  0.0 61.2 %shard_map.55 = f32[12,24,128]{2,1,0:T(8,128)S(1)} custom-call(bf16[12,24,128]{2,1,0:T(8,128)(2,1)} %pair_hbm.1, bf16[12,24,128]{2,1,0:T(8,128)(2,1)} %d_out_hbm.1, bf16[128,256]{1,0:T(8,128)(2,1)} %w_proj_hbm.1, bf16[128,128]{1,0:T(8,128)(2,1)} %w_gate_hbm.1, bf16[64,128]{1,0:T(8,128)(2,1)} %ow_hbm.1), custom_call_target="tpu_custom_call" | custom-call | tf_op jit(solution)/shard_map/pallas_call | solution.py:334
  61.2 0.7 %copy.7 = f32[12,24,128]{2,1,0:T(8,128)} copy(f32[12,24,128]{2,1,0:T(8,128)S(1)} %shard_map.55) | data formatting | bytes 294912

commit v7 on v6

--- a/solution.py
+++ b/solution.py
@@ -61,33 +61,37 @@
     pair_ref, d_out_ref, w_proj_ref, w_gate_ref, ow_ref,
     pad_ref, slots_ref, rows_ref, left_ref, right_ref,
     send_a, recv_a, send_b, recv_b, send_d, recv_d, send_e, recv_e, send_f, recv_f, send_g, recv_g, send_h, recv_h,
-    in_sem, send_sem, recv_sem, across_sem,
+    in_sem, send_sem, recv_sem, right_sem, across_sem,
 ):
     r = lax.axis_index("row")
     c = lax.axis_index("col")
     peer = lax.rem(r, PEERS)
     x_me = lax.rem(c, 4)
     z_lo = r // PEERS
-    z_me = (c // 4) * 4 + z_lo
+    z_hi = c // 4
+    z_me = z_hi * 4 + z_lo
     slot = (c // 4) * 16 + x_me * 4 + z_lo
+    order_x = [lax.rem(x_me + dx, 4) for dx in (2, 1, 3, 0)]
     barrier = pltpu.get_barrier_semaphore()
 
     def each_of_group(act):
-        def at(dz, dx):
+        def plane(dz, columns):
             z = lax.rem(z_me + dz, 16)
-            x = lax.rem(x_me + dx, 4)
-            act((lax.rem(z, 4) * PEERS + peer, (z // 4) * 4 + x), (z // 4) * 16 + x * 4 + lax.rem(z, 4))
+            high = lax.div(z, 4)
+            low = z - 4 * high
+            row = low * PEERS + peer
+            col = high * 4
+            base = high * 16 + low
+            for x in columns:
+                act((row, col + x), base + 4 * x)
 
         def step(n, carry):
-            away = (n + 1) // 2
-            dz = 8 + jnp.where(lax.rem(n, 2) == 1, away, -away)
-            for dx in (2, 1, 3, 0):
-                at(dz, dx)
+            away = lax.div(n + 1, 2)
+            plane(8 + jnp.where(lax.rem(n, 2) == 1, away, -away), order_x)
             return carry
 
         lax.fori_loop(0, 15, step, 0)
-        for dx in (2, 1, 3):
-            at(0, dx)
+        plane(0, order_x[:3])
 
     def each_peer(act):
         def step(d, carry):
@@ -96,12 +100,6 @@
             return carry
 
         lax.fori_loop(1, PEERS, step, 0)
-
-    def greet(device, _):
-        pl.semaphore_signal(barrier, inc=1, device_id=device, device_id_type=MESH)
-
-    each_of_group(greet)
-    each_peer(greet)
 
     loads = [
         pltpu.make_async_copy(src, dst, in_sem.at[n])
@@ -113,6 +111,12 @@
     for load in loads:
         load.start()
 
+    def greet(device, _):
+        pl.semaphore_signal(barrier, inc=1, device_id=device, device_id_type=MESH)
+
+    each_of_group(greet)
+    each_peer(greet)
+
     def wait_all(ref, sem):
         pltpu.make_async_copy(ref, ref, sem).wait()
 
@@ -127,6 +131,18 @@
         each_of_group(one)
         pltpu.make_async_copy(send.at[slot], recv.at[slot], recv_sem.at[phase]).start()
 
+    def exchange_right():
+        def one(device, to):
+            opposite = jnp.where(lax.rem(to // 16 + 4 - z_hi, 4) == 2, 1, 0)
+            pltpu.make_async_remote_copy(
+                src_ref=send_a.at[to], dst_ref=recv_a.at[slot],
+                send_sem=send_sem.at[0], recv_sem=right_sem.at[opposite],
+                device_id=device, device_id_type=MESH,
+            ).start()
+
+        each_of_group(one)
+        pltpu.make_async_copy(send_a.at[slot], recv_a.at[slot], right_sem.at[0]).start()
+
     def share(phase, src_of, recv):
         def one(device, to):
             pltpu.make_async_remote_copy(
@@ -137,24 +153,29 @@
 
         each_peer(one)
 
-    def move_right(block, to, send, recv):
+    sibling = peer + 1 - 2 * lax.rem(peer, 2)
+    nearer = [lax.rem(z_hi + away, 4) for away in (0, 1, 3)]
+    opposite = lax.rem(z_hi + 2, 4)
+
+    def move_right(block, zh, to, send, recv):
         pltpu.make_async_remote_copy(
-            src_ref=right_ref.at[block], dst_ref=right_ref.at[block], send_sem=send, recv_sem=recv,
+            src_ref=right_ref.at[block, zh], dst_ref=right_ref.at[block, zh], send_sem=send, recv_sem=recv,
             device_id=(z_lo * PEERS + to, c), device_id_type=MESH,
         ).start()
 
-    sibling = peer + 1 - 2 * lax.rem(peer, 2)
-
-    def start_across():
+    def start_across(parts, part):
         for d in (2, 1, 3):
-            move_right(peer, lax.rem(peer + 2 * d, PEERS), send_sem.at[2], across_sem.at[d])
-        move_right(peer, sibling, send_sem.at[9], recv_sem.at[2])
-
-    def to_sibling():
+            for zh in parts:
+                move_right(peer, zh, lax.rem(peer + 2 * d, PEERS), send_sem.at[2], across_sem.at[d, part])
+        for zh in parts:
+            move_right(peer, zh, sibling, send_sem.at[9], recv_sem.at[2])
+
+    def to_sibling(parts, part):
         for d in (1, 3, 2):
             block = lax.rem(peer + PEERS - 2 * d, PEERS)
-            wait_all(right_ref.at[block], across_sem.at[d])
-            move_right(block, sibling, send_sem.at[9], recv_sem.at[2])
+            wait_all(right_ref.at[block, pl.ds(0, len(parts))], across_sem.at[d, part])
+            for zh in parts:
+                move_right(block, zh, sibling, send_sem.at[9], recv_sem.at[2])
 
     def wait_sends(phase, ref):
         wait_all(ref.at[pl.ds(0, ref.shape[0] - 1)], send_sem.at[phase])
@@ -180,21 +201,23 @@
             slots_ref[4 * n : 4 * n + 4, :] = recv[n].astype(F32)
         return jnp.concatenate([slots_ref[pl.ds(a, GROUP, stride=4), :] for a in range(TILES)], axis=1)
 
-    def gather_rows(recv):
-        for zh in range(4):
-            for pair in range(2):
-                parts = []
-                for x in range(4):
-                    first = 16 * zh + 4 * x + 2 * pair
-                    parts.append(jnp.concatenate([recv[first].astype(F32), recv[first + 1].astype(F32)], axis=0))
-                for b, part in enumerate(swap_blocks(parts)):
-                    rows_ref[zh, pl.ds(32 * pair + b, 8, stride=4), :] = part
-            for zl in range(3):
-                rows_ref[zh, 16 * zl + HALF : 16 * zl + 16, :] = rows_ref[zh, 48 + 4 * zl : 52 + 4 * zl, :]
-        return close_gaps([rows_ref[zh, :48, :] for zh in range(4)])
-
-    def scatter_rows(array, send):
-        for zh, tile in enumerate(open_gaps([tile_of(array, t) for t in range(TILES)])):
+    def gather_block(recv, zh):
+        for pair in range(2):
+            parts = []
+            for x in range(4):
+                first = 16 * zh + 4 * x + 2 * pair
+                parts.append(jnp.concatenate([recv[first].astype(F32), recv[first + 1].astype(F32)], axis=0))
+            for b, part in enumerate(swap_blocks(parts)):
+                rows_ref[zh, pl.ds(32 * pair + b, 8, stride=4), :] = part
+        for zl in range(3):
+            rows_ref[zh, 16 * zl + HALF : 16 * zl + 16, :] = rows_ref[zh, 48 + 4 * zl : 52 + 4 * zl, :]
+
+    def keep_block(recv, zh, ref):
+        gather_block(recv, zh)
+        ref[peer, zh] = rows_ref[zh, :48, :].astype(BF16).reshape(3, 16, LANES)
+
+    def scatter_rows(tiles, send):
+        for zh, tile in enumerate(tiles):
             rows_ref[zh, :48, :] = tile
             for zl in range(3):
                 rows_ref[zh, 48 + 4 * zl : 52 + 4 * zl, :] = rows_ref[zh, 16 * zl + HALF : 16 * zl + 16, :]
@@ -205,14 +228,17 @@
                     send[first] = part[:4].astype(BF16)
                     send[first + 1] = part[4:].astype(BF16)
 
+    def tiles_of(array):
+        return [tile_of(array, t) for t in range(array.shape[1] // LANES)]
+
     def rows_of(ref, g):
-        return jnp.concatenate([ref[g, :, t].reshape(48, LANES) for t in range(TILES)], axis=1)
+        return jnp.concatenate([ref[g, zh].reshape(48, LANES) for zh in range(4)], axis=1)
 
     def all_rows(ref):
         return jnp.concatenate(
             [
-                jnp.concatenate([ref[:, zl, t].reshape(128, LANES) for zl in range(3)], axis=0)
-                for t in range(TILES)
+                jnp.concatenate([ref[:, zh, zl].reshape(128, LANES) for zl in range(3)], axis=0)
+                for zh in range(4)
             ],
             axis=1,
         )
@@ -233,7 +259,7 @@
     to_slots(right_gate * right_value, send_a)
 
     pl.semaphore_wait(barrier, GROUP - 1 + PEERS - 1)
-    exchange(0, send_a, recv_a)
+    exchange_right()
 
     projected = dot(w_rows[:128], normed)
     left_gate = jax.nn.sigmoid(projected[:64])
@@ -251,19 +277,23 @@
     d_xhat_mean = jnp.mean(d_xhat, axis=0, keepdims=True)
     gate_slope = upstream * gate * (1.0 - gate)
 
-    wait_all(recv_a, recv_sem.at[0])
-    for t, tile in enumerate(gather_rows(recv_a)):
-        right_ref[peer, :, t] = tile.astype(BF16).reshape(3, 16, LANES)
-    start_across()
+    wait_all(recv_a.at[pl.ds(0, 48)], right_sem.at[0])
+    for zh in nearer:
+        keep_block(recv_a, zh, right_ref)
+    start_across(nearer, 0)
+    wait_all(recv_a.at[pl.ds(0, 16)], right_sem.at[1])
+    keep_block(recv_a, opposite, right_ref)
+    start_across([opposite], 1)
+    to_sibling(nearer, 0)
     wait_all(recv_b, recv_sem.at[1])
-    for t, tile in enumerate(gather_rows(recv_b)):
-        left_ref[peer, :, t] = tile.astype(BF16).reshape(3, 16, LANES)
-    to_sibling()
+    for zh in range(4):
+        keep_block(recv_b, zh, left_ref)
+    to_sibling([opposite], 1)
     wait_sends(0, send_a)
     wait_sends(1, send_b)
     wait_all(right_ref.at[pl.ds(0, 4)], recv_sem.at[2])
     right = all_rows(right_ref)
-    scatter_rows(dot_t(rows_of(left_ref, peer), right), send_d)
+    scatter_rows(open_gaps(tiles_of(dot_t(rows_of(left_ref, peer), right))), send_d)
     exchange(4, send_d, recv_d)
     share(3, lambda to: left_ref.at[peer], left_ref)
     wait_all(right_ref.at[pl.ds(0, 3)], send_sem.at[2])
@@ -275,7 +305,6 @@
     x_inv = lax.rsqrt(jnp.mean(x_centre * x_centre, axis=0, keepdims=True) + EPS)
     xhat = x_centre * x_inv
     d_x = (d_xhat - d_xhat_mean - xhat * jnp.mean(d_xhat * xhat, axis=0, keepdims=True)) * x_inv
-    slots_ref[...] = jnp.zeros_like(slots_ref)
     to_slots(d_x, send_e)
     exchange(5, send_e, recv_e)
 
@@ -286,7 +315,9 @@
     wait_sends(4, send_d)
 
     wait_all(recv_e, recv_sem.at[5])
-    d_x_rows = jnp.concatenate(gather_rows(recv_e), axis=1)
+    for zh in range(4):
+        gather_block(recv_e, zh)
+    d_x_rows = jnp.concatenate(close_gaps([rows_ref[zh, :48, :] for zh in range(4)]), axis=1)
     padded = jnp.concatenate([d_x_rows, jnp.zeros((80, CELLS), F32)], axis=0)
     d_x_cols = padded.T.astype(BF16).reshape(3, PEERS, 16, LANES)
     for to in range(PEERS):
@@ -294,7 +325,7 @@
     recv_f[peer] = send_f[peer]
     share(6, lambda to: send_f.at[to], recv_f)
 
-    scatter_rows(dot(d_x_rows.astype(BF16), right), send_g)
+    scatter_rows(tiles_of(dot(d_x_rows.astype(BF16), right)), send_g)
     exchange(7, send_g, recv_g)
     wait_sends(5, send_e)
     wait_all(left_ref.at[pl.ds(0, PEERS - 1)], recv_sem.at[3])
@@ -303,7 +334,7 @@
     for g in range(PEERS):
         term = dot(recv_f[g].reshape(48, LANES)[:, :48], rows_of(left_ref, g))
         d_right = term if d_right is None else d_right + term
-    scatter_rows(d_right, send_h)
+    scatter_rows(tiles_of(d_right), send_h)
     exchange(8, send_h, recv_h)
 
     def back(grad, gates, vals, columns):
@@ -319,16 +350,16 @@
     d_normed += back(from_slots(recv_h), right_gate, right_value, w_proj_ref[:, 128:])
     grad_mean = jnp.mean(d_normed, axis=0, keepdims=True)
     cross_mean = jnp.mean(d_normed * zhat, axis=0, keepdims=True)
-    pad_ref[...] = ((d_normed - grad_mean - zhat * cross_mean) * inv_std).T
+    d_pair = ((d_normed - grad_mean - zhat * cross_mean) * inv_std).T
     for i in range(TILE_I):
-        out_ref[i, :HALF, :] = pad_ref[32 * i : 32 * i + HALF, :]
-        out_ref[i, HALF:, :] = pad_ref[32 * i + 16 : 32 * i + 16 + HALF, :]
+        out_ref[i, :HALF, :] = d_pair[32 * i : 32 * i + HALF]
+        out_ref[i, HALF:, :] = d_pair[32 * i + 16 : 32 * i + 16 + HALF]
     wait_sends(8, send_h)
 
 
 def per_device(pair, d_out, w_proj, w_gate, output_weight):
     slots = pltpu.VMEM((GROUP, 4, LANES), BF16)
-    rows = pltpu.VMEM((PEERS, 3, TILES, 16, LANES), BF16)
+    rows = pltpu.VMEM((PEERS, 4, 3, 16, LANES), BF16)
     blocks = pltpu.VMEM((PEERS, 3, 16, LANES), BF16)
     args = (pair, d_out, w_proj, w_gate, output_weight)
     return pl.pallas_call(
@@ -352,7 +383,8 @@
             pltpu.SemaphoreType.DMA((5,)),
             pltpu.SemaphoreType.DMA((10,)),
             pltpu.SemaphoreType.DMA((9,)),
-            pltpu.SemaphoreType.DMA((4,)),
+            pltpu.SemaphoreType.DMA((2,)),
+            pltpu.SemaphoreType.DMA((4, 2)),
         ],
         compiler_params=pltpu.CompilerParams(
             collective_id=0, has_side_effects=True, vmem_limit_bytes=48 * 1024 * 1024

time: 62.1 us -> 61.5 us (level)
  no operation moved by 1% of the time
where the time goes in v7:
time: 61.5 us; the launch traced here: 61.3 us
  Pallas kernels  60.6 us (99%)
  local copies, waits for them, and re-layouts  0.66 us (1%)
    pallas_call x1, Pallas kernels, per_device(): pl.pallas_call(body, out_shape=jax.ShapeDtypeStruct(pair.shape, F32), in_...  60.6 us

profile of v7, /device:TPU:1, one launch (start us, length us, event | category | flops | bytes accessed | tf_op | source)
XLA Modules:
  0.0 61.3 jit_solution(11214379058804279666)
XLA Ops:
  0.0 60.6 %shard_map.55 = f32[12,24,128]{2,1,0:T(8,128)S(1)} custom-call(bf16[12,24,128]{2,1,0:T(8,128)(2,1)} %pair_hbm.1, bf16[12,24,128]{2,1,0:T(8,128)(2,1)} %d_out_hbm.1, bf16[128,256]{1,0:T(8,128)(2,1)} %w_proj_hbm.1, bf16[128,128]{1,0:T(8,128)(2,1)} %w_gate_hbm.1, bf16[64,128]{1,0:T(8,128)(2,1)} %ow_hbm.1), custom_call_target="tpu_custom_call" | custom-call | tf_op jit(solution)/shard_map/pallas_call | solution.py:365
  60.7 0.7 %copy.7 = f32[12,24,128]{2,1,0:T(8,128)} copy(f32[12,24,128]{2,1,0:T(8,128)S(1)} %shard_map.55) | data formatting | bytes 294912

commit v8 on v7

--- a/solution.py
+++ b/solution.py
@@ -61,7 +61,7 @@
     pair_ref, d_out_ref, w_proj_ref, w_gate_ref, ow_ref,
     pad_ref, slots_ref, rows_ref, left_ref, right_ref,
     send_a, recv_a, send_b, recv_b, send_d, recv_d, send_e, recv_e, send_f, recv_f, send_g, recv_g, send_h, recv_h,
-    in_sem, send_sem, recv_sem, right_sem, across_sem,
+    in_sem, send_sem, recv_sem, right_sem, d_x_sem, across_sem,
 ):
     r = lax.axis_index("row")
     c = lax.axis_index("col")
@@ -131,17 +131,17 @@
         each_of_group(one)
         pltpu.make_async_copy(send.at[slot], recv.at[slot], recv_sem.at[phase]).start()
 
-    def exchange_right():
+    def exchange_split(phase, send, recv, sem):
         def one(device, to):
             opposite = jnp.where(lax.rem(to // 16 + 4 - z_hi, 4) == 2, 1, 0)
             pltpu.make_async_remote_copy(
-                src_ref=send_a.at[to], dst_ref=recv_a.at[slot],
-                send_sem=send_sem.at[0], recv_sem=right_sem.at[opposite],
+                src_ref=send.at[to], dst_ref=recv.at[slot],
+                send_sem=send_sem.at[phase], recv_sem=sem.at[opposite],
                 device_id=device, device_id_type=MESH,
             ).start()
 
         each_of_group(one)
-        pltpu.make_async_copy(send_a.at[slot], recv_a.at[slot], right_sem.at[0]).start()
+        pltpu.make_async_copy(send.at[slot], recv.at[slot], sem.at[0]).start()
 
     def share(phase, src_of, recv):
         def one(device, to):
@@ -259,7 +259,7 @@
     to_slots(right_gate * right_value, send_a)
 
     pl.semaphore_wait(barrier, GROUP - 1 + PEERS - 1)
-    exchange_right()
+    exchange_split(0, send_a, recv_a, right_sem)
 
     projected = dot(w_rows[:128], normed)
     left_gate = jax.nn.sigmoid(projected[:64])
@@ -306,7 +306,7 @@
     xhat = x_centre * x_inv
     d_x = (d_xhat - d_xhat_mean - xhat * jnp.mean(d_xhat * xhat, axis=0, keepdims=True)) * x_inv
     to_slots(d_x, send_e)
-    exchange(5, send_e, recv_e)
+    exchange_split(5, send_e, recv_e, d_x_sem)
 
     mixed = dot(ow_t, xhat.astype(BF16))
     d_gate = (mixed * gate_slope).astype(BF16)
@@ -314,9 +314,11 @@
     wait_sends(3, left_ref)
     wait_sends(4, send_d)
 
-    wait_all(recv_e, recv_sem.at[5])
-    for zh in range(4):
+    wait_all(recv_e.at[pl.ds(0, 48)], d_x_sem.at[0])
+    for zh in nearer:
         gather_block(recv_e, zh)
+    wait_all(recv_e.at[pl.ds(0, 16)], d_x_sem.at[1])
+    gather_block(recv_e, opposite)
     d_x_rows = jnp.concatenate(close_gaps([rows_ref[zh, :48, :] for zh in range(4)]), axis=1)
     padded = jnp.concatenate([d_x_rows, jnp.zeros((80, CELLS), F32)], axis=0)
     d_x_cols = padded.T.astype(BF16).reshape(3, PEERS, 16, LANES)
@@ -370,8 +372,8 @@
         scratch_shapes=[
             *(pltpu.VMEM(a.shape, a.dtype) for a in args),
             pltpu.VMEM((CELLS, LANES), F32),
-            pltpu.VMEM((GROUP * 4, LANES), F32),
-            pltpu.VMEM((4, 64, LANES), F32),
+            pltpu.VMEM((GROUP * 4 + 8, LANES), F32),
+            pltpu.VMEM((4, 72, LANES), F32),
             rows, rows,
             slots, slots,
             slots, slots,
@@ -383,6 +385,7 @@
             pltpu.SemaphoreType.DMA((5,)),
             pltpu.SemaphoreType.DMA((10,)),
             pltpu.SemaphoreType.DMA((9,)),
+            pltpu.SemaphoreType.DMA((2,)),
             pltpu.SemaphoreType.DMA((2,)),
             pltpu.SemaphoreType.DMA((4, 2)),
         ],

time: 61.5 us -> 61.5 us (level)
  no operation moved by 1% of the time
where the time goes in v8:
time: 61.5 us; the launch traced here: 61.4 us
  Pallas kernels  60.7 us (99%)
  local copies, waits for them, and re-layouts  0.66 us (1%)
    pallas_call x1, Pallas kernels, per_device(): pl.pallas_call(body, out_shape=jax.ShapeDtypeStruct(pair.shape, F32), in_...  60.7 us

profile of v8, /device:TPU:1, one launch (start us, length us, event | category | flops | bytes accessed | tf_op | source)
XLA Modules:
  0.0 61.4 jit_solution(16822743019555747305)
XLA Ops:
  0.0 60.7 %shard_map.55 = f32[12,24,128]{2,1,0:T(8,128)S(1)} custom-call(bf16[12,24,128]{2,1,0:T(8,128)(2,1)} %pair_hbm.1, bf16[12,24,128]{2,1,0:T(8,128)(2,1)} %d_out_hbm.1, bf16[128,256]{1,0:T(8,128)(2,1)} %w_proj_hbm.1, bf16[128,128]{1,0:T(8,128)(2,1)} %w_gate_hbm.1, bf16[64,128]{1,0:T(8,128)(2,1)} %ow_hbm.1), custom_call_target="tpu_custom_call" | custom-call | tf_op jit(solution)/shard_map/pallas_call | solution.py:367
  60.7 0.7 %copy.7 = f32[12,24,128]{2,1,0:T(8,128)} copy(f32[12,24,128]{2,1,0:T(8,128)S(1)} %shard_map.55) | data formatting | bytes 294912

commit v9 on v8

--- a/solution.py
+++ b/solution.py
@@ -181,10 +181,11 @@
         wait_all(ref.at[pl.ds(0, ref.shape[0] - 1)], send_sem.at[phase])
 
     def padded_transpose(ref):
-        for i in range(TILE_I):
-            cells = ref[i].astype(F32)
-            pad_ref[32 * i : 32 * i + HALF, :] = cells[:HALF]
-            pad_ref[32 * i + 16 : 32 * i + 16 + HALF, :] = cells[HALF:]
+        for pair in range(TILE_I // 2):
+            cells = ref[4 * HALF * pair : 4 * HALF * (pair + 1), :].astype(F32)
+            for half in range(4):
+                at = 64 * pair + 16 * half
+                pad_ref[at : at + HALF, :] = cells[HALF * half : HALF * (half + 1)]
         return pad_ref[...].T
 
     def tile_of(array, t):
@@ -363,7 +364,7 @@
     slots = pltpu.VMEM((GROUP, 4, LANES), BF16)
     rows = pltpu.VMEM((PEERS, 4, 3, 16, LANES), BF16)
     blocks = pltpu.VMEM((PEERS, 3, 16, LANES), BF16)
-    args = (pair, d_out, w_proj, w_gate, output_weight)
+    args = (pair.reshape(-1, LANES), d_out.reshape(-1, LANES), w_proj, w_gate, output_weight)
     return pl.pallas_call(
         body,
         out_shape=jax.ShapeDtypeStruct(pair.shape, F32),

time: 61.5 us -> 61.5 us (level)
  no operation moved by 1% of the time
where the time goes in v9:
time: 61.5 us; the launch traced here: 61.4 us
  Pallas kernels  60.7 us (99%)
  local copies, waits for them, and re-layouts  0.66 us (1%)
    pallas_call x1, Pallas kernels, per_device(): pl.pallas_call(body, out_shape=jax.ShapeDtypeStruct(pair.shape, F32), in_...  60.7 us

profile of v9, /device:TPU:1, one launch (start us, length us, event | category | flops | bytes accessed | tf_op | source)
XLA Modules:
  0.0 61.4 jit_solution(16822743019555747305)
XLA Ops:
  0.0 60.7 %shard_map.55 = f32[12,24,128]{2,1,0:T(8,128)S(1)} custom-call(bf16[288,128]{1,0:T(8,128)(2,1)} %bitcast.2, bf16[288,128]{1,0:T(8,128)(2,1)} %bitcast.3, bf16[128,256]{1,0:T(8,128)(2,1)} %w_proj_hbm.1, bf16[128,128]{1,0:T(8,128)(2,1)} %w_gate_hbm.1, bf16[64,128]{1,0:T(8,128)(2,1)} %ow_hbm.1), custom_call_target="tpu_custom_call" | custom-call | tf_op jit(solution)/shard_map/pallas_call | solution.py:368
  60.7 0.7 %copy.7 = f32[12,24,128]{2,1,0:T(8,128)} copy(f32[12,24,128]{2,1,0:T(8,128)S(1)} %shard_map.55) | data formatting | bytes 294912

commit v10 on v9

--- a/solution.py
+++ b/solution.py
@@ -94,12 +94,12 @@
         plane(0, order_x[:3])
 
     def each_peer(act):
-        def step(d, carry):
-            to = lax.rem(peer + d, PEERS)
-            act((z_lo * PEERS + to, c), to)
-            return carry
-
-        lax.fori_loop(1, PEERS, step, 0)
+        other_core = 1 - 2 * lax.rem(peer, 2)
+        for dy in (2, 1, 3):
+            to = lax.rem(peer + 2 * dy, PEERS)
+            for peer_to in (to, to + other_core):
+                act((z_lo * PEERS + peer_to, c), peer_to)
+        act((z_lo * PEERS + peer + other_core, c), peer + other_core)
 
     loads = [
         pltpu.make_async_copy(src, dst, in_sem.at[n])

time: 61.5 us -> 61.5 us (level)
  no operation moved by 1% of the time
where the time goes in v10:
time: 61.5 us; the launch traced here: 61.4 us
  Pallas kernels  60.7 us (99%)
  local copies, waits for them, and re-layouts  0.66 us (1%)
    pallas_call x1, Pallas kernels, per_device(): pl.pallas_call(body, out_shape=jax.ShapeDtypeStruct(pair.shape, F32), in_...  60.7 us

profile of v10, /device:TPU:1, one launch (start us, length us, event | category | flops | bytes accessed | tf_op | source)
XLA Modules:
  0.0 61.4 jit_solution(10221772166566204583)
XLA Ops:
  0.0 60.7 %shard_map.55 = f32[12,24,128]{2,1,0:T(8,128)S(1)} custom-call(bf16[288,128]{1,0:T(8,128)(2,1)} %bitcast.2, bf16[288,128]{1,0:T(8,128)(2,1)} %bitcast.3, bf16[128,256]{1,0:T(8,128)(2,1)} %w_proj_hbm.1, bf16[128,128]{1,0:T(8,128)(2,1)} %w_gate_hbm.1, bf16[64,128]{1,0:T(8,128)(2,1)} %ow_hbm.1), custom_call_target="tpu_custom_call" | custom-call | tf_op jit(solution)/shard_map/pallas_call | solution.py:368
  60.7 0.7 %copy.7 = f32[12,24,128]{2,1,0:T(8,128)} copy(f32[12,24,128]{2,1,0:T(8,128)S(1)} %shard_map.55) | data formatting | bytes 294912

commit v11 on v10

--- a/solution.py
+++ b/solution.py
@@ -391,7 +391,7 @@
             pltpu.SemaphoreType.DMA((4, 2)),
         ],
         compiler_params=pltpu.CompilerParams(
-            collective_id=0, has_side_effects=True, vmem_limit_bytes=48 * 1024 * 1024
+            collective_id=0, has_side_effects=True, skip_device_barrier=True, vmem_limit_bytes=48 * 1024 * 1024
         ),
     )(*(pltpu.with_memory_space_constraint(a, pltpu.HBM) for a in args))
 

time: 61.5 us -> 61.5 us (level)
  no operation moved by 1% of the time
where the time goes in v11:
time: 61.5 us; the launch traced here: 61.4 us
  Pallas kernels  60.7 us (99%)
  local copies, waits for them, and re-layouts  0.66 us (1%)
    pallas_call x1, Pallas kernels, per_device(): pl.pallas_call(body, out_shape=jax.ShapeDtypeStruct(pair.shape, F32), in_...  60.7 us

profile of v11, /device:TPU:1, one launch (start us, length us, event | category | flops | bytes accessed | tf_op | source)
XLA Modules:
  0.0 61.4 jit_solution(10221772166566204583)
XLA Ops:
  0.0 60.7 %shard_map.55 = f32[12,24,128]{2,1,0:T(8,128)S(1)} custom-call(bf16[288,128]{1,0:T(8,128)(2,1)} %bitcast.2, bf16[288,128]{1,0:T(8,128)(2,1)} %bitcast.3, bf16[128,256]{1,0:T(8,128)(2,1)} %w_proj_hbm.1, bf16[128,128]{1,0:T(8,128)(2,1)} %w_gate_hbm.1, bf16[64,128]{1,0:T(8,128)(2,1)} %ow_hbm.1), custom_call_target="tpu_custom_call" | custom-call | tf_op jit(solution)/shard_map/pallas_call | solution.py:368
  60.7 0.7 %copy.7 = f32[12,24,128]{2,1,0:T(8,128)} copy(f32[12,24,128]{2,1,0:T(8,128)S(1)} %shard_map.55) | data formatting | bytes 294912
